TPU v7x, 32 devices: a whole 2x2x4 slice. The times are simulated.
32 devices in a mesh: dp: 16 (over z, y, x), head: 2 (over core).
Axes of the slice: x: 2, y: 2, z: 4, core: 2. Of those that a mesh axis runs over, the one named last changes fastest.
Arguments:
- tokens: bfloat16 [50176, 384], P('dp'), may hold values from -6 to 6
- keep: int32 [256, 2], P('dp'), may hold values 0 or 1
- cotangent: bfloat16 [50176, 384], P(('dp', 'head')), may hold values from -6 to 6
- input_weight: float32 [3, 384, 384], P(None, 'dp', 'head'), may hold values from -0.3125 to 0.3125
- output_weight: float32 [384, 384], P('head', 'dp'), may hold values from -1.25 to 1.25
- expand_weight: float32 [384, 1536], P(None, ('dp', 'head')), may hold values from -0.3125 to 0.3125
- shrink_weight: float32 [1536, 384], P(('dp', 'head')), may hold values from -0.15625 to 0.15625
- bias_tables: float32 [12, 530], P('head'), may hold values from -4 to 4
- vectors: float32 [12, 384], replicated, may hold values from -0.6 to 1.6
- first_input: float32 [3, 384, 384], P(None, 'dp', 'head'), may hold values from -80 to 80
- second_input: float32 [3, 384, 384], P(None, 'dp', 'head'), may hold values from 6.272 to 100.352
- average_input: float32 [3, 384, 384], P(None, 'dp', 'head'), may hold values from -0.3125 to 0.3125
- first_output: float32 [384, 384], P('head', 'dp'), may hold values from -40 to 40
- second_output: float32 [384, 384], P('head', 'dp'), may hold values from 1.568 to 25.088
- average_output: float32 [384, 384], P('head', 'dp'), may hold values from -1.25 to 1.25
- first_expand: float32 [384, 1536], P(None, ('dp', 'head')), may hold values from -80 to 80
- second_expand: float32 [384, 1536], P(None, ('dp', 'head')), may hold values from 6.272 to 100.352
- average_expand: float32 [384, 1536], P(None, ('dp', 'head')), may hold values from -0.3125 to 0.3125
- first_shrink: float32 [1536, 384], P(('dp', 'head')), may hold values from -80 to 80
- second_shrink: float32 [1536, 384], P(('dp', 'head')), may hold values from 6.272 to 100.352
- average_shrink: float32 [1536, 384], P(('dp', 'head')), may hold values from -0.15625 to 0.15625
- first_tables: float32 [12, 530], P('head'), may hold values from -16 to 16
- second_tables: float32 [12, 530], P('head'), may hold values from 0.25088 to 4.01408
- average_tables: float32 [12, 530], P('head'), may hold values from -4 to 4
- first_vectors: float32 [12, 384], replicated, may hold values from -160 to 160
- second_vectors: float32 [12, 384], replicated, may hold values from 25.088 to 401.408
- average_vectors: float32 [12, 384], replicated, may hold values from -0.6 to 1.6
Outputs:
- result: float32 [50176, 384], P(('dp', 'head'))
- input_grad: float32 [50176, 384], P(('dp', 'head'))
- input_new: float32 [3, 384, 384], P(None, 'dp', 'head')
- input_first: float32 [3, 384, 384], P(None, 'dp', 'head')
- input_second: float32 [3, 384, 384], P(None, 'dp', 'head')
- input_average: float32 [3, 384, 384], P(None, 'dp', 'head')
- input_copy: bfloat16 [3, 384, 384], P(None, 'dp', 'head')
- output_new: float32 [384, 384], P('head', 'dp')
- output_first: float32 [384, 384], P('head', 'dp')
- output_second: float32 [384, 384], P('head', 'dp')
- output_average: float32 [384, 384], P('head', 'dp')
- output_copy: bfloat16 [384, 384], P('head', 'dp')
- expand_new: float32 [384, 1536], P(None, ('dp', 'head'))
- expand_first: float32 [384, 1536], P(None, ('dp', 'head'))
- expand_second: float32 [384, 1536], P(None, ('dp', 'head'))
- expand_average: float32 [384, 1536], P(None, ('dp', 'head'))
- expand_copy: bfloat16 [384, 1536], P(None, ('dp', 'head'))
- shrink_new: float32 [1536, 384], P(('dp', 'head'))
- shrink_first: float32 [1536, 384], P(('dp', 'head'))
- shrink_second: float32 [1536, 384], P(('dp', 'head'))
- shrink_average: float32 [1536, 384], P(('dp', 'head'))
- shrink_copy: bfloat16 [1536, 384], P(('dp', 'head'))
- tables_new: float32 [12, 530], P('head')
- tables_first: float32 [12, 530], P('head')
- tables_second: float32 [12, 530], P('head')
- tables_average: float32 [12, 530], P('head')
- vectors_new: float32 [12, 384], replicated
- vectors_first: float32 [12, 384], replicated
- vectors_second: float32 [12, 384], replicated
- vectors_average: float32 [12, 384], replicated
All inputs are finite; a program needn't handle non-finite values. No bound on the sum of `keep` on one device may be relied on, other than what follows from the above.
Results may differ from a plain program's by a relative error of at most 0.014.
The roundings to bfloat16 on the way count: a program that leaves them out, or rounds other values in their place, can miss the bound.
Values may be sent and summed in bfloat16 or wider, within the bound.
No kernel may reach another device: no remote copies, remote signals or barrier semaphores. Data moves between devices by JAX's collectives and lax.ppermute only.
A program may use at most 384 MiB of HBM per device.

v0:
```python
from functools import partial

import jax
import jax.numpy as jnp
import numpy as np
from jax import lax
from jax.sharding import PartitionSpec as P

HEAD_DIM = 32
SIDE = 14
WINDOW = 7
FINE = 13
STEP = 10


DROP_SCALE = 1.25


def shortened(x):

    def short(part):
        return part.astype(jnp.bfloat16) if part.dtype == jnp.float32 else part

    return jax.tree.map(short, x)


def build_toolkit():

    def value_plain(v):
        return lax.optimization_barrier(v.astype(jnp.bfloat16)).astype(jnp.float32)

    round_value = jax.custom_vjp(value_plain)

    def value_keep(v):
        return (round_value(v), None)

    def value_pass(kept, grad):
        return (grad,)

    round_value.defvjp(value_keep, value_pass)

    def grad_plain(v):
        return v

    round_grad = jax.custom_vjp(grad_plain)

    def grad_keep(v):
        return (v, None)

    def grad_narrow(kept, grad):
        return (round_value(grad),)

    round_grad.defvjp(grad_keep, grad_narrow)

    def product_plain(form, left_form, right_form, scale, left, right):
        return scale * jnp.einsum(
            form,
            left.astype(jnp.bfloat16),
            right.astype(jnp.bfloat16),
            preferred_element_type=jnp.float32,
        )

    product = jax.custom_vjp(product_plain, nondiff_argnums=(0, 1, 2, 3))

    def product_keep(form, left_form, right_form, scale, left, right):
        return (product(form, left_form, right_form, scale, left, right), (left, right))

    def product_back(form, left_form, right_form, scale, kept, grad):
        left, right = kept
        narrow = grad.astype(jnp.bfloat16)
        grad_left = scale * jnp.einsum(
            left_form, narrow, right.astype(jnp.bfloat16), preferred_element_type=jnp.float32
        )
        grad_right = scale * jnp.einsum(
            right_form, left.astype(jnp.bfloat16), narrow, preferred_element_type=jnp.float32
        )
        return (grad_left, grad_right)

    product.defvjp(product_keep, product_back)
    return (round_value, round_grad, product)


def matmul(toolkit, left, right):
    return toolkit[2]("nd,de->ne", "ne,de->nd", "nd,ne->de", 1.0, left, right)


def focal_tables():
    half = SIDE // 2
    across = SIDE // WINDOW
    margin = (FINE - WINDOW) // 2
    span = WINDOW + FINE - 1
    coarse_span = SIDE - 1
    cells = np.arange(WINDOW * WINDOW)
    query_row = cells // WINDOW
    query_col = cells % WINDOW
    places = np.arange(FINE * FINE)
    key_row = places // FINE
    key_col = places % FINE
    near_index = (key_row[None, :] - query_row[:, None] + WINDOW - 1) * span + (
        key_col[None, :] - query_col[:, None] + WINDOW - 1
    )
    pooled = np.arange(half * half)
    pool_row = pooled // half
    pool_col = pooled % half
    index_list = []
    mask_list = []
    for row in range(across):
        for col in range(across):
            row_abs = row * WINDOW + query_row
            col_abs = col * WINDOW + query_col
            far_index = (
                span * span
                + (row_abs[:, None] // 2 - pool_row[None, :] + half - 1) * coarse_span
                + (col_abs[:, None] // 2 - pool_col[None, :] + half - 1)
            )
            index_list.append(np.concatenate([near_index, far_index], axis=1))
            key_row_abs = row * WINDOW - margin + key_row
            key_col_abs = col * WINDOW - margin + key_col
            inside = (
                (key_row_abs >= 0)
                & (key_row_abs < SIDE)
                & (key_col_abs >= 0)
                & (key_col_abs < SIDE)
            )
            mask_list.append(
                np.concatenate([np.where(inside, 0.0, -1000000000.0), np.zeros(half * half)])
            )
    return (np.stack(index_list).astype(np.int32), np.stack(mask_list).astype(np.float32))


def attend(toolkit, mixed, table):
    round_value, round_grad, product = toolkit
    count = mixed.shape[1] // (SIDE * SIDE)
    heads = table.shape[0]
    half = SIDE // 2
    across = SIDE // WINDOW
    windows = across * across
    margin = (FINE - WINDOW) // 2
    maps = mixed.reshape(3, count, SIDE, SIDE, heads, HEAD_DIM)
    query = round_value(maps[0])
    pooled = round_value(
        jnp.mean(maps[1:].reshape(2, count, half, 2, half, 2, heads, HEAD_DIM), axis=(3, 5))
    )
    fine = jnp.pad(
        round_value(maps[1:]), ((0, 0), (0, 0), (margin, margin), (margin, margin), (0, 0), (0, 0))
    )
    blocks = [
        fine[:, :, row * WINDOW : row * WINDOW + FINE, col * WINDOW : col * WINDOW + FINE]
        for row in range(across)
        for col in range(across)
    ]
    near = jnp.stack(blocks, axis=2).reshape(2, count, windows, FINE * FINE, heads, HEAD_DIM)
    far = jnp.broadcast_to(
        pooled.reshape(2, count, 1, half * half, heads, HEAD_DIM),
        (2, count, windows, half * half, heads, HEAD_DIM),
    )
    context = jnp.concatenate([near, far], axis=3)
    queries = query.reshape(count, across, WINDOW, across, WINDOW, heads, HEAD_DIM).transpose(
        0, 1, 3, 2, 4, 5, 6
    )
    queries = queries.reshape(count, windows, WINDOW * WINDOW, heads, HEAD_DIM)
    index, blocked = focal_tables()
    bias = jnp.transpose(table[:, index], (1, 0, 2, 3))
    scores = product(
        "bwqhd,bwkhd->bwhqk",
        "bwhqk,bwkhd->bwqhd",
        "bwqhd,bwhqk->bwkhd",
        HEAD_DIM ** (-0.5),
        queries,
        context[0],
    )
    scores = round_grad(scores + bias[None] + blocked[None, :, None, None, :])
    top = jnp.max(scores, axis=-1, keepdims=True)
    weights = jnp.exp(scores - top)
    probs = round_value(weights / jnp.sum(weights, axis=-1, keepdims=True))
    attended = product(
        "bwhqk,bwkhd->bwqhd", "bwqhd,bwkhd->bwhqk", "bwhqk,bwqhd->bwkhd", 1.0, probs, context[1]
    )
    attended = attended.reshape(count, across, across, WINDOW, WINDOW, heads, HEAD_DIM).transpose(
        0, 1, 3, 2, 4, 5, 6
    )
    return attended.reshape(count * SIDE * SIDE, heads * HEAD_DIM)


def layer_norm(stream, gain, shift):
    center = stream - jnp.mean(stream, axis=-1, keepdims=True)
    spread = jnp.mean(center * center, axis=-1, keepdims=True)
    return center * lax.rsqrt(spread + 1e-05) * gain + shift


def attn_local(toolkit, normed, w_in, query_bias, value_bias, w_out, table):
    round_value, round_grad, product = toolkit
    bias = jnp.stack([query_bias, jnp.zeros_like(query_bias), value_bias])
    mixed = product("nd,tdc->tnc", "tnc,tdc->nd", "nd,tnc->tdc", 1.0, normed, w_in)
    mixed = round_grad(mixed + bias[:, None, :])
    attended = round_grad(round_value(attend(toolkit, mixed, table)))
    return round_grad(matmul(toolkit, attended, w_out))


def mlp_local(toolkit, normed, w_expand, expand_bias, w_shrink):
    round_value, round_grad, product = toolkit
    pre = round_grad(matmul(toolkit, normed, w_expand) + expand_bias)
    act = round_value(jax.nn.gelu(pre, approximate=False))
    return round_grad(matmul(toolkit, act, w_shrink))


def adamw(weight, grad, first, second, average, rate, decay):
    first = 0.9 * first + 0.1 * grad
    second = 0.999 * second + 0.001 * grad * grad
    fix_one = 1.0 - 0.9**STEP
    fix_two = 1.0 - 0.999**STEP
    weight = weight - rate * (
        first / fix_one / (jnp.sqrt(second / fix_two) + 1e-08) + decay * weight
    )
    average = 0.9 * average + 0.1 * weight
    return (weight, first, second, average)


def shards(
    tokens,
    keep,
    cotangent,
    input_weight,
    output_weight,
    expand_weight,
    shrink_weight,
    bias_tables,
    vectors,
    first_input,
    second_input,
    average_input,
    first_output,
    second_output,
    average_output,
    first_expand,
    second_expand,
    average_expand,
    first_shrink,
    second_shrink,
    average_shrink,
    first_tables,
    second_tables,
    average_tables,
    first_vectors,
    second_vectors,
    average_vectors,
):
    toolkit = build_toolkit()
    round_value = toolkit[0]
    attn_apply = partial(attn_local, toolkit)
    mlp_apply = partial(mlp_local, toolkit)
    head_index = lax.axis_index("head")
    head_count = lax.axis_size("head")
    width = vectors.shape[1]
    local_width = input_weight.shape[2]
    local_heads = bias_tables.shape[0]
    image_rows = SIDE * SIDE
    own_rows = cotangent.shape[0]
    own_images = own_rows // image_rows
    part_in, part_out = (
        lax.all_gather(input_weight.astype(jnp.bfloat16), "dp", axis=1, tiled=True),
        lax.all_gather(output_weight.astype(jnp.bfloat16), "dp", axis=1, tiled=True),
    )
    use_in, use_out = (part_in, part_out)
    query_bias = lax.dynamic_slice_in_dim(vectors[2], head_index * local_width, local_width, 0)
    value_bias = lax.dynamic_slice_in_dim(vectors[3], head_index * local_width, local_width, 0)
    expand_full, shrink_full = (
        lax.all_gather(expand_weight.astype(jnp.bfloat16), ("dp", "head"), axis=1, tiled=True),
        lax.all_gather(shrink_weight.astype(jnp.bfloat16), ("dp", "head"), axis=0, tiled=True),
    )
    expand_bias = vectors[8:].reshape(-1)
    stream = tokens.astype(jnp.float32)
    own_stream = lax.dynamic_slice_in_dim(stream, head_index * own_rows, own_rows, 0)
    normed = round_value(layer_norm(stream, vectors[0], vectors[1]))
    partial_branch, attn_pull = jax.vjp(
        attn_apply,
        normed,
        use_in.astype(jnp.float32),
        query_bias,
        value_bias,
        use_out.astype(jnp.float32),
        bias_tables,
    )
    branch = jax.tree.map(
        lambda part: part.astype(jnp.float32),
        lax.psum_scatter(shortened(partial_branch), "head", scatter_dimension=0, tiled=True),
    )
    flags = lax.dynamic_slice_in_dim(keep, head_index * own_images, own_images, 0).astype(
        jnp.float32
    )
    keep_attn = jnp.repeat(flags[:, 0], image_rows)[:, None]
    keep_mlp = jnp.repeat(flags[:, 1], image_rows)[:, None]
    state = own_stream + keep_attn * DROP_SCALE * (branch + vectors[4])
    normed_two, norm_two_pull = jax.vjp(layer_norm, state, vectors[5], vectors[6])
    normed_two = round_value(normed_two)
    mlp_out, mlp_pull = jax.vjp(
        mlp_apply,
        normed_two,
        expand_full.astype(jnp.float32),
        expand_bias,
        shrink_full.astype(jnp.float32),
    )
    result = state + keep_mlp * DROP_SCALE * (mlp_out + vectors[7])
    upstream = cotangent.astype(jnp.float32)
    mlp_scaled = keep_mlp * DROP_SCALE * upstream
    mlp_signal = round_value(mlp_scaled)
    grad_rows, grad_expand, grad_expand_bias, grad_shrink = mlp_pull(mlp_signal)
    grad_from_norm, grad_gain_two, grad_shift_two = norm_two_pull(grad_rows)
    grad_state = upstream + grad_from_norm
    attn_scaled = keep_attn * DROP_SCALE * grad_state
    attn_signal = round_value(attn_scaled)
    signal_rows = lax.all_gather(
        attn_signal.astype(jnp.bfloat16), "head", axis=0, tiled=True
    ).astype(jnp.float32)
    grad_normed, grad_in, grad_query_bias, grad_value_bias, grad_out, grad_table = attn_pull(
        signal_rows
    )
    grad_normed_own = jax.tree.map(
        lambda part: part.astype(jnp.float32),
        lax.psum_scatter(shortened(grad_normed), "head", scatter_dimension=0, tiled=True),
    )
    unused_normed, norm_one_pull = jax.vjp(layer_norm, own_stream, vectors[0], vectors[1])
    grad_own, grad_gain_one, grad_shift_one = norm_one_pull(grad_normed_own)
    input_grad = grad_state + grad_own
    grad_in_shard, grad_out_shard = (
        lax.psum_scatter(grad_in, "dp", scatter_dimension=1, tiled=True),
        lax.psum_scatter(grad_out, "dp", scatter_dimension=1, tiled=True),
    )
    grad_expand_shard, grad_shrink_shard = (
        lax.psum_scatter(grad_expand, ("dp", "head"), scatter_dimension=1, tiled=True),
        lax.psum_scatter(grad_shrink, ("dp", "head"), scatter_dimension=0, tiled=True),
    )
    zero_row = jnp.zeros((width,), jnp.float32)
    query_row = lax.dynamic_update_slice_in_dim(
        zero_row, grad_query_bias, head_index * local_width, 0
    )
    value_row = lax.dynamic_update_slice_in_dim(
        zero_row, grad_value_bias, head_index * local_width, 0
    )
    table_full = lax.dynamic_update_slice_in_dim(
        jnp.zeros((local_heads * head_count, bias_tables.shape[1]), jnp.float32),
        grad_table,
        head_index * local_heads,
        0,
    )
    vector_rows = jnp.stack(
        [
            grad_gain_one,
            grad_shift_one,
            query_row,
            value_row,
            jnp.sum(attn_scaled, axis=0),
            grad_gain_two,
            grad_shift_two,
            jnp.sum(mlp_scaled, axis=0),
        ]
    )
    vector_grad = jnp.concatenate([vector_rows, grad_expand_bias.reshape(-1, width)], axis=0)
    vector_total, table_total = lax.psum((vector_grad, table_full), ("dp", "head"))
    table_grad = lax.dynamic_slice_in_dim(table_total, head_index * local_heads, local_heads, 0)
    input_new = adamw(
        input_weight, grad_in_shard, first_input, second_input, average_input, 0.06, 0.05
    )
    output_new = adamw(
        output_weight, grad_out_shard, first_output, second_output, average_output, 0.3, 0.05
    )
    expand_new = adamw(
        expand_weight, grad_expand_shard, first_expand, second_expand, average_expand, 0.06, 0.05
    )
    shrink_new = adamw(
        shrink_weight, grad_shrink_shard, first_shrink, second_shrink, average_shrink, 0.06, 0.05
    )
    tables_new = adamw(
        bias_tables, table_grad, first_tables, second_tables, average_tables, 1.0, 0.0
    )
    vectors_new = adamw(
        vectors, vector_total, first_vectors, second_vectors, average_vectors, 0.6, 0.0
    )
    return (
        result,
        input_grad,
        input_new[0],
        input_new[1],
        input_new[2],
        input_new[3],
        input_new[0].astype(jnp.bfloat16),
        output_new[0],
        output_new[1],
        output_new[2],
        output_new[3],
        output_new[0].astype(jnp.bfloat16),
        expand_new[0],
        expand_new[1],
        expand_new[2],
        expand_new[3],
        expand_new[0].astype(jnp.bfloat16),
        shrink_new[0],
        shrink_new[1],
        shrink_new[2],
        shrink_new[3],
        shrink_new[0].astype(jnp.bfloat16),
        tables_new[0],
        tables_new[1],
        tables_new[2],
        tables_new[3],
        vectors_new[0],
        vectors_new[1],
        vectors_new[2],
        vectors_new[3],
    )


def solution(mesh):
    in_specs = (
        P("dp", None),
        P("dp", None),
        P(("dp", "head"), None),
        P(None, "dp", "head"),
        P("head", "dp"),
        P(None, ("dp", "head")),
        P(("dp", "head"), None),
        P("head", None),
        P(),
        P(None, "dp", "head"),
        P(None, "dp", "head"),
        P(None, "dp", "head"),
        P("head", "dp"),
        P("head", "dp"),
        P("head", "dp"),
        P(None, ("dp", "head")),
        P(None, ("dp", "head")),
        P(None, ("dp", "head")),
        P(("dp", "head"), None),
        P(("dp", "head"), None),
        P(("dp", "head"), None),
        P("head", None),
        P("head", None),
        P("head", None),
        P(),
        P(),
        P(),
    )
    out_specs = (
        P(("dp", "head"), None),
        P(("dp", "head"), None),
        P(None, "dp", "head"),
        P(None, "dp", "head"),
        P(None, "dp", "head"),
        P(None, "dp", "head"),
        P(None, "dp", "head"),
        P("head", "dp"),
        P("head", "dp"),
        P("head", "dp"),
        P("head", "dp"),
        P("head", "dp"),
        P(None, ("dp", "head")),
        P(None, ("dp", "head")),
        P(None, ("dp", "head")),
        P(None, ("dp", "head")),
        P(None, ("dp", "head")),
        P(("dp", "head"), None),
        P(("dp", "head"), None),
        P(("dp", "head"), None),
        P(("dp", "head"), None),
        P(("dp", "head"), None),
        P("head", None),
        P("head", None),
        P("head", None),
        P("head", None),
        P(),
        P(),
        P(),
        P(),
    )
    return jax.shard_map(shards, mesh=mesh, in_specs=in_specs, out_specs=out_specs, check_vma=False)
```

profile of v0, /device:TPU:1, one launch (start us, length us, event | category | flops | bytes accessed | tf_op | source)
XLA Modules:
  0.0 1505.4 jit_solution(4913278252295997758)
XLA Ops:
  15.7 38.2 %all_gather.15 = bf16[3,384,192]{2,1,0:T(8,128)(2,1)S(1)} all-gather(bf16[3,24,192]{2,1,0:T(8,128)(2,1)S(1)} %convert_element_type.198), channel_id=1, replica_groups=mesh['dp'=16,'head'=2] {'dp'}, dimensions={1}, use_global_device_ids=true | all-gather | bytes 470016 | tf_op jit(solution)/shard_map/all_gather | solution.py:261
  65.5 32.0 %all_gather.16 = bf16[192,384]{0,1:T(8,128)(2,1)} all-gather(bf16[192,24]{0,1:T(8,128)(2,1)S(1)} %convert_element_type.214), channel_id=1, replica_groups=mesh['dp'=16,'head'=2] {'dp'}, dimensions={1}, use_global_device_ids=true | all-gather | bytes 156672 | tf_op jit(solution)/shard_map/all_gather | solution.py:262
  115.4 8.2 copy.236
  130.0 14.2 convert_element_type.200
  144.2 13.7 pad_convert_fusion
  157.9 28.9 %fusion.57 = (bf16[2,16,13,13,6,32]{5,4,3,2,1,0:T(8,128)(2,1)}, bf16[2,16,13,13,6,32]{5,4,3,2,1,0:T(8,128)(2,1)}, bf16[2,16,13,13,6,32]{5,4,3,2,1,0:T(8,128)(2,1)}, bf16[2,16,13,13,6,32]{5,4,3,2,1,0:T(8,128)(2,1)}) fusion(bf16[2,16,20,20,6,32]{5,4,3,2,1,0:T(8,128)(2,1)} %pad_convert_fusion), kind=kLoop, calls=%fused_computation.169 | loop fusion | bytes 16613376 | tf_op jit(solution)/shard_map/jvp()/slice | solution.py:148
  186.9 11.8 copy.227
  198.7 11.8 copy.230
  210.5 11.8 copy.229
  222.3 11.8 copy.228
  234.1 15.5 %reshape.261 = f32[2,16,7,2,7,2,6,32]{7,6,5,4,3,2,1,0:T(8,128)} reshape(f32[2,3136,192]{2,1,0:T(8,128)} %copy.231) | data formatting | bytes 9633792 | tf_op jit(solution)/shard_map/jvp()/reshape | solution.py:142
  249.6 13.9 reduce_sum.223
  274.3 86.5 %gather_fusion = f32[42728,6]{1,0:T(8,128)} fusion(f32[6,530]{0,1:T(8,128)S(1)} %copy.238, s32[43008]{0:T(1024)} %pad_clamp_fusion), kind=kCustom, calls=%fused_computation | custom fusion | bytes 2221856 | tf_op jit(solution)/shard_map/jvp()/gather | solution.py:163
  360.7 12.6 copy.239
  380.3 11.0 maximum_convert_fusion
  391.3 12.7 fusion.1
  404.7 13.5 fusion.37
  418.2 18.4 %convert_reduce_fusion.1 = (f32[16,4,6,49]{3,2,1,0:T(8,128)}, pred[16,4,6,49,218]{4,3,2,1,0:T(8,128)(4,1)}, bf16[16,4,6,49,218]{4,3,2,1,0:T(8,128)(2,1)}) fusion(f32[16,4,6,49]{3,2,1,0:T(8,128)} %copy-done.18, f32[4,218]{1,0:T(4,128)S(1)} %copy-done.36, f32[16,4,6,49,218]{4,3,2,1,0:T(8,128)} %get-tuple-element.198, f32[16,4,6,49]{3,2,1,0:T(8,128)S(1)} %fusion.37, ...), kind=kLoop, calls=%fused_computation.8 | loop fusion | flops 36898176 | bytes 29967968 | tf_op jit(solution)/shard_map/jvp()/reduce_sum | solution.py:173
  442.4 8.9 copy.241
  458.0 8.3 convert_element_type.213
  476.5 15.7 %reduce-scatter.6.cloned.1.call-done = bf16[1568,384]{1,0:T(8,128)(2,1)} async-done(((bf16[3136,384]{1,0:T(8,128)(2,1)}), bf16[1568,384]{1,0:T(8,128)(2,1)}) %reduce-scatter.6.cloned.1.call-update) | async-done | bytes 1204240 | tf_op jit(solution)/shard_map/reduce_scatter | solution.py:286
  497.8 42.9 %all-gather.4.cloned.1.call-done = bf16[384,1536]{0,1:T(8,128)(2,1)} async-done(((bf16[384,48]{0,1:T(8,128)(2,1)}), bf16[384,1536]{0,1:T(8,128)(2,1)}) %all-gather.4.cloned.1.call-update) | async-done | bytes 1179664 | tf_op jit(solution)/shard_map/all_gather | solution.py:268
  540.6 26.1 %multiply_convert_fusion = (bf16[1568,1536]{1,0:T(8,128)(2,1)S(1)}, f32[1568,1536]{1,0:T(8,128)}, f32[1568,1536]{1,0:T(8,128)}) fusion(f32[1536]{0:T(1024)S(1)} %add.316, bf16[1568,384]{1,0:T(8,128)(2,1)} %add_convert_fusion.4, bf16[384,1536]{0,1:T(8,128)(2,1)} %all-gather.4.cloned.1.call-done), kind=kOutput, calls=%fused_computation.31 | convolution fusion | flops 2008645632 | bytes 26474496 | tf_op jit(solution)/shard_map/jvp(nd,de->ne)/dot_general | solution.py:56
  573.3 95.8 %reduce-scatter.14.cloned.1.call-done = f32[48,384]{1,0:T(8,128)} async-done(((f32[1536,384]{1,0:T(8,128)}), f32[48,384]{1,0:T(8,128)}) %reduce-scatter.14.cloned.1.call-update) | async-done | bytes 73744 | tf_op jit(solution)/shard_map/reduce_scatter | solution.py:331
  670.9 56.9 %all-gather.6.cloned.1.call-done = bf16[1536,384]{1,0:T(8,128)(2,1)} async-done(((bf16[48,384]{1,0:T(8,128)(2,1)}), bf16[1536,384]{1,0:T(8,128)(2,1)}) %all-gather.6.cloned.1.call-update) | async-done | bytes 1179664 | tf_op jit(solution)/shard_map/all_gather | solution.py:269
  727.8 11.1 add_convert_fusion.2
  748.4 9.2 all-gather.8.cloned.1.call-done
  792.4 11.0 convolution_bitcast_fusion.1
  803.5 23.7 %multiply_reduce_fusion = (f32[16,4,6,49]{3,2,1,0:T(8,128)S(1)}, f32[16,4,6,49,218]{4,3,2,1,0:T(8,128)}) fusion(f32[16,4,6,49]{3,2,1,0:T(8,128)S(1)} %copy-done.24, f32[16,4,6,49]{3,2,1,0:T(8,128)S(1)} %copy-done.19, f32[4,218]{1,0:T(4,128)S(1)} %copy-done.37, f32[16,4,6,49,218]{4,3,2,1,0:T(8,128)} %get-tuple-element.198, ...), kind=kOutput, calls=%fused_computation.10 | convolution fusion | flops 291215232 | bytes 47178080 | tf_op jit(solution)/shard_map/transpose(jvp(bwqhd,bwkhd->bwhqk))/dot_general | solution.py:176
  827.3 22.6 %fusion.52 = (f32[16,4,6,49]{3,2,1,0:T(8,128)S(1)}, f32[16,4,6,49,218]{4,3,2,1,0:T(8,128)}) fusion(f32[16,4,6,49]{3,2,1,0:T(8,128)S(1)} %copy-done.19, f32[4,218]{1,0:T(4,128)S(1)} %copy-done.37, f32[16,4,6,49,218]{4,3,2,1,0:T(8,128)} %get-tuple-element.198, f32[16,4,6,49]{3,2,1,0:T(8,128)S(1)} %neg.25, f32[16,4,6,49,218]{4,3,2,1,0:T(8,128)} %get-tuple-element.202, ...), kind=kLoop, calls=%fused_computation.166 | loop fusion | flops 32796288 | bytes 50552672 | tf_op jit(solution)/shard_map/transpose(jvp())/reduce_sum | solution.py:174
  849.9 10.7 add_convert_fusion.1
  860.7 10.3 multiply_bitcast_fusion.1
  876.9 10.0 fusion.2
  886.9 14.9 slice_add_fusion
  901.8 46.0 %copy.277 = f32[2,16,4,169,6,32]{5,1,4,3,0,2:T(8,128)} copy(f32[2,16,4,169,6,32]{3,5,4,2,1,0:T(8,128)} %slice_add_fusion) | data formatting | bytes 33226752 | tf_op jit(solution)/shard_map/transpose(jvp())/reshape | solution.py:152
  947.8 46.0 %copy.248 = f32[2,16,4,169,6,32]{5,1,4,3,2,0:T(8,128)} copy(f32[2,16,4,169,6,32]{3,5,4,2,1,0:T(8,128)} %slice_add_fusion) | data formatting | bytes 33226752 | tf_op jit(solution)/shard_map/transpose(jvp())/split | solution.py:157
  1002.7 11.1 copy.253
  1013.8 8.7 copy.254
  1022.5 34.0 %slice_bitcast_fusion.3 = (f32[2,16,13,13,6,32]{5,1,4,3,2,0:T(8,128)}, f32[2,16,13,13,6,32]{5,1,4,3,2,0:T(8,128)}, f32[2,16,13,13,6,32]{5,1,4,3,2,0:T(8,128)}) fusion(f32[2,16,4,13,13,6,32]{6,1,5,4,3,0,2:T(8,128)} %bitcast.136), kind=kLoop, calls=%fused_computation.20 | loop fusion | bytes 24920064 | tf_op jit(solution)/shard_map/transpose(jvp())/unstack | solution.py:152
  1056.5 13.4 slice_bitcast_fusion
  1073.2 18.0 %pad_add_fusion = f32[2,16,14,14,6,32]{5,1,4,3,2,0:T(8,128)} fusion(f32[2,16,13,13,6,32]{5,1,4,3,2,0:T(8,128)} %slice_bitcast_fusion, f32[2,16,13,13,6,32]{5,1,4,3,2,0:T(8,128)} %get-tuple-element.173, f32[2,16,13,13,6,32]{5,1,4,3,2,0:T(8,128)} %get-tuple-element.174, f32[2,16,13,13,6,32]{5,1,4,3,2,0:T(8,128)S(1)} %bitcast.140), kind=kLoop, calls=%fused_computation.14 | loop fusion | flops 3612672 | bytes 21430272 | tf_op jit(solution)/shard_map/transpose(jvp())/add_any | solution.py:148
  1091.1 11.5 broadcast_in_dim.83
  1102.7 21.6 %add_convert_fusion = bf16[3,16,14,14,6,32]{5,1,4,3,2,0:T(8,128)(2,1)} fusion(f32[1,16,14,14,6,32]{5,1,4,3,2,0:T(8,128)} %bitcast.145, f32[2,16,14,14,6,32]{5,1,4,3,2,0:T(8,128)} %bitcast.138, f32[2,16,14,14,6,32]{5,1,4,3,2,0:T(8,128)} %pad_add_fusion), kind=kLoop, calls=%fused_computation.2 | loop fusion | flops 5419008 | bytes 15654912 | tf_op jit(solution)/shard_map/transpose(jvp())/convert_element_type | solution.py:195
  1124.2 12.9 copy.255
  1137.1 22.3 %convert_element_type.232 = bf16[3,3136,192]{2,1,0:T(8,128)(2,1)} reshape(bf16[3,16,14,14,6,32]{5,4,3,2,1,0:T(8,128)(2,1)} %copy.255) | data formatting | bytes 7225344 | tf_op jit(solution)/shard_map/transpose(jvp())/convert_element_type | solution.py:195
  1192.2 11.4 copy.264
  1203.6 229.6 %scatter_custom_fusion = f32[6,530]{0,1:T(8,128)S(1)} fusion(s32[42728]{0:T(1024)} %constant.254, f32[42728,6]{1,0:T(8,128)} %copy.264, f32[]{:T(128)} %constant.71.clone.1), kind=kCustom, calls=%fused_computation.101 | custom fusion | flops 256368 | bytes 13232 | tf_op jit(solution)/shard_map/transpose(jvp())/scatter-add | solution.py:163
  1451.0 40.0 %all-reduce.11 = (f32[12,530]{1,0:T(8,128)S(1)}, f32[12,384]{1,0:T(8,128)S(1)}) all-reduce(f32[12,530]{1,0:T(8,128)S(1)} %dynamic_update_slice.11, f32[12,384]{1,0:T(8,128)S(1)} %concatenate.8), channel_id=1, replica_groups=mesh['dp'=16,'head'=2] {'dp','head'}, use_global_device_ids=true, to_apply=%region_25.26 | all-reduce | flops 10968 | bytes 87744 | tf_op jit(solution)/shard_map/psum | solution.py:359
  (312 shorter events, 216.6 us)
Async XLA Ops:
  8.0 45.9 %copy-start.7 = (bf16[3136,384]{1,0:T(8,128)(2,1)S(1)}, bf16[3136,384]{1,0:T(8,128)(2,1)}, u32[]{:S(2)}) copy-start(bf16[3136,384]{1,0:T(8,128)(2,1)} %param.30) | copy-start | bytes 7225348
  8.0 484.1 %reduce-scatter.6.cloned.1.call-start = ((), (), s32[]{:S(2)}) async-start(), calls=%async_computation.5 | async-start | bytes 3612672 | tf_op jit(solution)/shard_map/reduce_scatter | solution.py:286
  9.7 44.2 %copy-start.59 = (f32[384]{0:T(512)}, f32[384]{0:T(512)S(1)}, u32[]{:S(2)}) copy-start(f32[384]{0:T(512)S(1)} %get-tuple-element.185) | copy-start | bytes 4612
  62.3 35.2 %copy-start.42 = (f32[6,530]{1,0:T(8,128)S(1)}, f32[6,530]{1,0:T(8,128)}, u32[]{:S(2)}) copy-start(f32[6,530]{1,0:T(8,128)} %param.37) | copy-start | bytes 38164
  130.0 261.3 %copy-start.2 = (bf16[16,4,49,6,32]{2,4,3,1,0:T(8,128)(2,1)}, bf16[16,4,49,6,32]{2,4,3,1,0:T(8,128)(2,1)S(1)}, u32[]{:S(2)}) copy-start(bf16[16,4,49,6,32]{2,4,3,1,0:T(8,128)(2,1)S(1)} %copy.237) | copy-start | bytes 3612676
  404.7 31.9 %slice-start = ((s8[12582912]{0:T(1024)(128)(4,1)}), s8[4194304]{0:T(1024)(128)(4,1)S(1)}, s32[]{:S(2)}) async-start(s8[12582912]{0:T(1024)(128)(4,1)} %bitcast.134), calls=%async_computation.14 | async-start | bytes 8388608
  404.7 31.9 %slice-start.1 = ((s8[12582912]{0:T(1024)(128)(4,1)}), s8[4194304]{0:T(1024)(128)(4,1)S(1)}, s32[]{:S(2)}) async-start(s8[12582912]{0:T(1024)(128)(4,1)} %bitcast.134), calls=%async_computation.15 | async-start | bytes 8388608
  418.2 329.5 %copy-start.23 = (f32[16,4,6,49]{3,2,1,0:T(8,128)}, f32[16,4,6,49]{3,2,1,0:T(8,128)S(1)}, u32[]{:S(2)}) copy-start(f32[16,4,6,49]{3,2,1,0:T(8,128)S(1)} %fusion.37) | copy-start | bytes 225796
  470.1 70.5 %all-gather.4.cloned.1.call-start = ((), (), s32[]{:S(2)}) async-start(), calls=%async_computation.6 | async-start | bytes 1216512 | tf_op jit(solution)/shard_map/all_gather | solution.py:268
  470.9 198.3 %reduce-scatter.14.cloned.1.call-start = ((), (), s32[]{:S(2)}) async-start(), calls=%async_computation.12 | async-start | bytes 2433024 | tf_op jit(solution)/shard_map/reduce_scatter | solution.py:331
  473.7 270.1 %copy-start.47 = (f32[1568]{0:T(1024)}, f32[1568]{0:T(1024)S(1)}, u32[]{:S(2)}) copy-start(f32[1568]{0:T(1024)S(1)} %mul.521) | copy-start | bytes 18820
  495.7 247.1 %copy-start.9 = (f32[1568,384]{1,0:T(8,128)}, f32[1568,384]{1,0:T(8,128)S(1)}, u32[]{:S(2)}) copy-start(f32[1568,384]{1,0:T(8,128)S(1)} %get-tuple-element.171) | copy-start | bytes 7225348
  568.8 100.3 %copy-start.49 = (f32[48,384]{1,0:T(8,128)S(1)}, f32[48,384]{1,0:T(8,128)}, u32[]{:S(2)}) copy-start(f32[48,384]{1,0:T(8,128)} %param.36) | copy-start | bytes 221188
  568.8 100.3 %copy-start.50 = (f32[48,384]{1,0:T(8,128)S(1)}, f32[48,384]{1,0:T(8,128)}, u32[]{:S(2)}) copy-start(f32[48,384]{1,0:T(8,128)} %param.48) | copy-start | bytes 221188
  568.8 100.3 %copy-start.51 = (f32[48,384]{1,0:T(8,128)S(1)}, f32[48,384]{1,0:T(8,128)}, u32[]{:S(2)}) copy-start(f32[48,384]{1,0:T(8,128)} %param.49) | copy-start | bytes 221188
  573.3 154.5 %all-gather.6.cloned.1.call-start = ((), (), s32[]{:S(2)}) async-start(), calls=%async_computation.7 | async-start | bytes 1216512 | tf_op jit(solution)/shard_map/all_gather | solution.py:269
  670.8 86.8 %all-gather.8.cloned.1.call-start = ((), (), s32[]{:S(2)}) async-start(), calls=%async_computation.8 | async-start | bytes 3612672 | tf_op jit(solution)/shard_map/all_gather | solution.py:312
  747.6 690.3 %reduce-scatter.10.cloned.1.call-start = ((), (), s32[]{:S(2)}) async-start(), calls=%async_computation.10 | async-start | bytes 417792 | tf_op jit(solution)/shard_map/reduce_scatter | solution.py:327
  761.1 678.8 %reduce-scatter.12.cloned.1.call-start = ((), (), s32[]{:S(2)}) async-start(), calls=%async_computation.11 | async-start | bytes 2433024 | tf_op jit(solution)/shard_map/reduce_scatter | solution.py:330
  768.0 674.2 %all-reduce.14.cloned.1.call-start = ((), (), s32[]{:S(2)}) async-start(), calls=%async_computation.13 | async-start | bytes 3145728
  947.8 46.0 %copy-start.13 = (f32[2,16,49,6,32]{2,4,3,1,0:T(8,128)S(1)}, f32[2,16,49,6,32]{2,4,3,1,0:T(8,128)}, u32[]{:S(2)}) copy-start(f32[2,16,49,6,32]{2,4,3,1,0:T(8,128)} %fusion.2) | copy-start | bytes 3612676
  1165.6 278.9 %reduce-scatter.8.cloned.1.call-start = ((), (), s32[]{:S(2)}) async-start(), calls=%async_computation.9 | async-start | bytes 3612672 | tf_op jit(solution)/shard_map/reduce_scatter | solution.py:320
  1192.1 245.8 %copy-start.40 = (f32[192,24]{0,1:T(8,128)S(1)}, f32[192,24]{0,1:T(8,128)}, u32[]{:S(2)}) copy-start(f32[192,24]{0,1:T(8,128)} %param.34) | copy-start | bytes 55300
  1192.1 245.8 %copy-start.66 = (f32[192,24]{0,1:T(8,128)S(1)}, f32[192,24]{0,1:T(8,128)}, u32[]{:S(2)}) copy-start(f32[192,24]{0,1:T(8,128)} %param.42) | copy-start | bytes 55300
  1192.1 245.8 %copy-start.67 = (f32[192,24]{0,1:T(8,128)S(1)}, f32[192,24]{0,1:T(8,128)}, u32[]{:S(2)}) copy-start(f32[192,24]{0,1:T(8,128)} %param.43) | copy-start | bytes 55300
  1192.1 247.2 %copy-start.65 = (f32[192,24]{0,1:T(8,128)S(1)}, f32[192,24]{0,1:T(8,128)}, u32[]{:S(2)}) copy-start(f32[192,24]{0,1:T(8,128)} %param.44) | copy-start | bytes 55300
  1192.2 247.8 %copy-start.34 = (f32[384,48]{0,1:T(8,128)S(1)}, f32[384,48]{0,1:T(8,128)}, u32[]{:S(2)}) copy-start(f32[384,48]{0,1:T(8,128)} %param.35) | copy-start | bytes 221188
  1192.2 247.8 %copy-start.52 = (f32[384,48]{0,1:T(8,128)S(1)}, f32[384,48]{0,1:T(8,128)}, u32[]{:S(2)}) copy-start(f32[384,48]{0,1:T(8,128)} %param.45) | copy-start | bytes 221188
  1192.2 247.7 %copy-start.53 = (f32[384,48]{0,1:T(8,128)S(1)}, f32[384,48]{0,1:T(8,128)}, u32[]{:S(2)}) copy-start(f32[384,48]{0,1:T(8,128)} %param.46) | copy-start | bytes 221188
  1203.6 237.9 %copy-start.57 = (f32[384,48]{0,1:T(8,128)S(1)}, f32[384,48]{0,1:T(8,128)}, u32[]{:S(2)}) copy-start(f32[384,48]{0,1:T(8,128)} %param.47) | copy-start | bytes 221188
  1203.6 239.5 %copy-start.35 = (f32[3,24,192]{2,1,0:T(8,128)S(1)}, f32[3,24,192]{2,1,0:T(8,128)}, u32[]{:S(2)}) copy-start(f32[3,24,192]{2,1,0:T(8,128)} %param.33) | copy-start | bytes 165892
  1203.6 239.5 %copy-start.54 = (f32[3,24,192]{2,1,0:T(8,128)S(1)}, f32[3,24,192]{2,1,0:T(8,128)}, u32[]{:S(2)}) copy-start(f32[3,24,192]{2,1,0:T(8,128)} %param.39) | copy-start | bytes 165892
  1203.6 239.5 %copy-start.55 = (f32[3,24,192]{2,1,0:T(8,128)S(1)}, f32[3,24,192]{2,1,0:T(8,128)}, u32[]{:S(2)}) copy-start(f32[3,24,192]{2,1,0:T(8,128)} %param.40) | copy-start | bytes 165892
  1203.6 240.2 %copy-start.58 = (f32[3,24,192]{2,1,0:T(8,128)S(1)}, f32[3,24,192]{2,1,0:T(8,128)}, u32[]{:S(2)}) copy-start(f32[3,24,192]{2,1,0:T(8,128)} %param.41) | copy-start | bytes 165892
  1203.6 240.8 %copy-start.60 = (f32[384]{0:T(512)S(1)}, f32[384]{0:T(512)}, u32[]{:S(2)}) copy-start(f32[384]{0:T(512)} %copy-done.59) | copy-start | bytes 4612
  1433.4 57.6 %copy-start.43 = (f32[6,530]{1,0:T(8,128)S(1)}, f32[6,530]{1,0:T(8,128)}, u32[]{:S(2)}) copy-start(f32[6,530]{1,0:T(8,128)} %param.37) | copy-start | bytes 38164
  1433.4 57.6 %copy-start.68 = (f32[6,530]{1,0:T(8,128)S(1)}, f32[6,530]{1,0:T(8,128)}, u32[]{:S(2)}) copy-start(f32[6,530]{1,0:T(8,128)} %param.53) | copy-start | bytes 38164
  1433.4 57.6 %copy-start.69 = (f32[6,530]{1,0:T(8,128)S(1)}, f32[6,530]{1,0:T(8,128)}, u32[]{:S(2)}) copy-start(f32[6,530]{1,0:T(8,128)} %param.51) | copy-start | bytes 38164
  1433.4 57.6 %copy-start.70 = (f32[6,530]{1,0:T(8,128)S(1)}, f32[6,530]{1,0:T(8,128)}, u32[]{:S(2)}) copy-start(f32[6,530]{1,0:T(8,128)} %param.52) | copy-start | bytes 38164
  1433.4 58.3 %copy-start.44 = (f32[12,384]{1,0:T(8,128)S(1)}, f32[12,384]{1,0:T(8,128)}, u32[]{:S(2)}) copy-start(f32[12,384]{1,0:T(8,128)} %param.38) | copy-start | bytes 55300
  1433.4 58.3 %copy-start.62 = (f32[12,384]{1,0:T(8,128)S(1)}, f32[12,384]{1,0:T(8,128)}, u32[]{:S(2)}) copy-start(f32[12,384]{1,0:T(8,128)} %param.56) | copy-start | bytes 55300
  1433.5 58.2 %copy-start.63 = (f32[12,384]{1,0:T(8,128)S(1)}, f32[12,384]{1,0:T(8,128)}, u32[]{:S(2)}) copy-start(f32[12,384]{1,0:T(8,128)} %param.54) | copy-start | bytes 55300
  1433.5 58.2 %copy-start.64 = (f32[12,384]{1,0:T(8,128)S(1)}, f32[12,384]{1,0:T(8,128)}, u32[]{:S(2)}) copy-start(f32[12,384]{1,0:T(8,128)} %param.55) | copy-start | bytes 55300
  1433.5 58.9 %copy-start.12 = (f32[1568,384]{1,0:T(8,128)S(1)}, f32[1568,384]{1,0:T(8,128)}, u32[]{:S(2)}) copy-start(f32[1568,384]{1,0:T(8,128)} %copy-done.11) | copy-start | bytes 7225348
  1433.5 58.9 %copy-start.46 = (f32[1568]{0:T(1024)S(1)}, f32[1568]{0:T(1024)}, u32[]{:S(2)}) copy-start(f32[1568]{0:T(1024)} %copy-done.45) | copy-start | bytes 18820
  1439.3 58.2 %copy-start.41 = (f32[192,24]{0,1:T(8,128)}, f32[192,24]{0,1:T(8,128)S(1)}, u32[]{:S(2)}) copy-start(f32[192,24]{0,1:T(8,128)S(1)} %get-tuple-element.155) | copy-start | bytes 55300
  1441.5 56.0 %copy-start.31 = (f32[384,48]{0,1:T(8,128)}, f32[384,48]{0,1:T(8,128)S(1)}, u32[]{:S(2)}) copy-start(f32[384,48]{0,1:T(8,128)S(1)} %get-tuple-element.151) | copy-start | bytes 221188
  1443.8 53.7 %copy-start.32 = (f32[3,24,192]{2,1,0:T(8,128)}, f32[3,24,192]{2,1,0:T(8,128)S(1)}, u32[]{:S(2)}) copy-start(f32[3,24,192]{2,1,0:T(8,128)S(1)} %get-tuple-element.159) | copy-start | bytes 165892
  (52 other events, 549.3 us)
Sparse Core Ops, SparseCore 0:
  470.3 21.8 reduce-scatter.5
  747.7 9.8 all-gather.7
  762.3 120.8 reduce-scatter.9
  889.1 98.1 reduce-scatter.11
  1165.7 117.6 all-reduce.13
  1286.1 10.3 reduce-scatter.7
Sparse Core Ops, SparseCore 1:
  474.5 66.1 all-gather.3
  573.4 95.8 reduce-scatter.13
  672.5 55.2 all-gather.5
where the time goes:
time: 1520 us; the launch traced here: 1510 us
  local copies, waits for them, and re-layouts  552 us (36%)
  other arithmetic  450 us (30%)
  waiting for transfers between devices  221 us (15%)
  matrix products  154 us (10%)
  blocking collectives  110 us (7%)
  between operations  17.9 us (1%)
    scatter-add x1, other arithmetic, attend(): bias = jnp.transpose(table[:, index], (1, 0, 2, 3))  230 us
    gather x3, local copies, waits for them, and re-layouts, attend(): bias = jnp.transpose(table[:, index], (1, 0, 2, 3))  103 us
    reduce_scatter x1, waiting for transfers between devices, shards(): lax.psum_scatter(grad_shrink, ('dp', 'head'), scatter_dimension=0, tiled=...  95.8 us
    another operation x6, local copies, waits for them, and re-layouts, attend(): jnp.stack(blocks, axis=2)  94.6 us
    dot_general x6, matrix products, product_plain(): jnp.einsum(form, left.astype(jnp.bfloat16), right.astype(jnp.bfloat16), p...  59.2 us
    all_gather x1, waiting for transfers between devices, shards(): lax.all_gather(shrink_weight.astype(jnp.bfloat16), ('dp', 'head'), axis=0...  56.9 us
    convert_element_type x6, local copies, waits for them, and re-layouts, value_plain(): return lax.optimization_barrier(v.astype(jnp.bfloat16)).astype(jnp.float32)  46.5 us
    split x1, local copies, waits for them, and re-layouts, attend(): context = jnp.concatenate([near, far], axis=3)  46 us
  transfers between devices with their start and end apart: 9, of which 5 were waited for; matrix products, arithmetic and copies ran while one was open for 46% of the time, Pallas kernels for 0%

commit v1 on v0

v1 whole, which is shorter than its diff:
```python
from functools import partial

import jax
import jax.numpy as jnp
import numpy as np
from jax import lax
from jax.experimental import pallas as pl
from jax.experimental.pallas import tpu as pltpu
from jax.sharding import PartitionSpec as P

HEAD_DIM = 32
SIDE = 14
WINDOW = 7
FINE = 13
STEP = 10
DROP_SCALE = 1.25

CELLS = SIDE * SIDE
HALF = SIDE // 2
POOL = HALF * HALF
SPAN = WINDOW + FINE - 1
FAR_SPAN = SIDE - 1
ROWS = 208
WIDE = 256
TOP = WINDOW * SIDE
OFFSET = CELLS - (WINDOW + (FINE - WINDOW) // 2) * SIDE
NEAR = CELLS - OFFSET
SLOTS = 192
LANES = 128
GROUP = LANES // HEAD_DIM
PAIR = 2
MANY = 4
SCALE = HEAD_DIM**-0.5
TO_LOG2 = SCALE * 1.4426950408889634
LINE = 384
CENTRE = 192
FAR_CENTRE = 64
FAR_ROW = NEAR // 8 * 8

BF = jnp.bfloat16
F32 = jnp.float32


def nn(a, b, **kw):
    return lax.dot_general(a, b, (((1,), (0,)), ((), ())), preferred_element_type=F32, **kw)


def nt(a, b, **kw):
    return lax.dot_general(a, b, (((1,), (1,)), ((), ())), preferred_element_type=F32, **kw)


def split(v):
    high = v.astype(BF)
    return high, (v - high.astype(F32)).astype(BF)


def cost(micros, bytes_accessed=0):
    return pl.CostEstimate(
        flops=int(micros * 1.15e9), bytes_accessed=bytes_accessed, transcendentals=0
    )


def params(mebibytes):
    return pltpu.CompilerParams(vmem_limit_bytes=mebibytes * 2**20)


def kinds():
    q = np.arange(CELLS)
    qr, qc = q // SIDE, q % SIDE
    margin = (FINE - WINDOW) // 2
    low_r, low_c = qr // WINDOW * WINDOW - margin, qc // WINDOW * WINDOW - margin
    key = np.arange(NEAR)[:, None] + np.where(q < TOP, 0, OFFSET)[None]
    kr, kc = key // SIDE, key % SIDE
    inside = (kr >= low_r) & (kr < low_r + FINE) & (kc >= low_c) & (kc < low_c + FINE)
    kind = np.zeros((SLOTS, WIDE), np.int32)
    kind[:NEAR, :CELLS] = np.where(inside, np.where(qc >= kc, 1, 2), 0)
    kind[NEAR : NEAR + POOL] = 3
    col = np.arange(POOL) % HALF
    far = np.zeros((SLOTS - FAR_ROW, LANES), np.int32)
    shift = NEAR - FAR_ROW
    far[shift : shift + POOL, :POOL] = np.where(col[None] >= col[:, None], 1, 2)
    spread = np.zeros((LANES, WIDE), np.float32)
    spread[qr // 2 * HALF + qc // 2, q] = 1.0
    return kind, far, spread


def pooling():
    rows = SLOTS - FAR_ROW
    shift = NEAR - FAR_ROW
    token = np.arange(CELLS)
    out = np.zeros((2 * rows, ROWS), np.float32)
    for half in range(2):
        for i in range(shift):
            out[rows * half + i, FAR_ROW + i + OFFSET * half] = 1.0
        out[rows * half + shift + token // SIDE // 2 * HALF + token % SIDE // 2, token] = 0.25
    return out


def head_rows():
    lane = np.arange(2 * LANES) % LANES // HEAD_DIM
    return (lane[None] == np.arange(8)[:, None]).astype(np.float32)


def table_lines(tables):
    heads = tables.shape[0]
    fine = tables[:, : SPAN * SPAN].reshape(heads, SPAN, SPAN)[:, ::-1, ::-1]
    far = tables[:, SPAN * SPAN :].reshape(heads, FAR_SPAN, FAR_SPAN)

    def lines(part, pitch, lanes, centre):
        reach = part.shape[1] // 2
        right = jnp.pad(part[:, :, reach:], ((0, 0), (0, 0), (0, pitch - reach - 1)))
        left = jnp.pad(part[:, :, :reach], ((0, 0), (0, 0), (pitch - reach, 0)))
        start = centre - pitch * reach
        size = pitch * part.shape[1]
        right = jnp.pad(right.reshape(heads, size), ((0, 0), (start, lanes - start - size)))
        start = start - pitch
        left = jnp.pad(left.reshape(heads, size), ((0, 0), (start, lanes - start - size)))
        return right, left

    both = lines(fine, SIDE, LINE, CENTRE) + lines(far, HALF, LANES, FAR_CENTRE)
    return jnp.concatenate(both, axis=1)


def table_from_lines(right, left, far_right, far_left):
    heads = right.shape[0]

    def part(right, left, count, pitch, centre):
        reach = count // 2
        start = centre - pitch * reach
        size = pitch * count
        right = right[:, start : start + size].reshape(heads, count, pitch)[:, :, : reach + 1]
        start = start - pitch
        left = left[:, start : start + size].reshape(heads, count, pitch)[:, :, pitch - reach :]
        return jnp.concatenate([left, right], axis=2)

    fine = part(right, left, SPAN, SIDE, CENTRE)[:, ::-1, ::-1]
    far = part(far_right, far_left, FAR_SPAN, HALF, FAR_CENTRE)
    return jnp.concatenate([fine.reshape(heads, -1), far.reshape(heads, -1)], axis=1)


def spread_kernel(line_ref, kind_ref, far_kind_ref, spread_ref, out_ref):
    kind = kind_ref[...]
    far_kind = far_kind_ref[...]
    tiles = FAR_ROW // 8 + 1
    down = OFFSET // 8
    near_kind = kind[: 8 * tiles]
    lower = lax.broadcasted_iota(jnp.int32, (8, WIDE), 1) >= TOP
    shift = FAR_CENTRE + NEAR - FAR_ROW
    far_tiles = far_kind_ref.shape[0] // 8

    def stacked(part, tiles, centre, lanes):
        size = part.shape[1]
        base = pltpu.roll(jnp.broadcast_to(part, (8, size)), 0, 1, stride=1, stride_axis=0)
        return [pltpu.roll(base, (8 * t - centre) % size, 1)[:, :lanes] for t in range(tiles)]

    for h in range(GROUP):
        line = line_ref[0, h : h + 1]
        sides = []
        for start in (0, LINE):
            rolled = stacked(line[:, start : start + LINE], tiles + down, CENTRE, WIDE)
            sides.append(
                jnp.concatenate(
                    [jnp.where(lower, rolled[t + down], rolled[t]) for t in range(tiles)], axis=0
                )
            )
        fine = jnp.where(near_kind == 1, sides[0], jnp.where(near_kind == 2, sides[1], -1e9))
        far_line = line[:, 2 * LINE :]
        far_right = jnp.concatenate(stacked(far_line[:, :LANES], far_tiles, shift, LANES), axis=0)
        far_left = jnp.concatenate(stacked(far_line[:, LANES:], far_tiles, shift, LANES), axis=0)
        far = jnp.where(far_kind == 1, far_right, jnp.where(far_kind == 2, far_left, 0.0))
        far = nn(far, spread_ref[...], precision=lax.Precision.HIGHEST)
        rest = jnp.concatenate(
            [fine[FAR_ROW:], jnp.full((SLOTS - 8 * tiles, WIDE), -1e9, F32)], axis=0
        )
        out_ref[h, :FAR_ROW] = fine[:FAR_ROW] * (1.0 / SCALE)
        out_ref[h, FAR_ROW:] = jnp.where(kind[FAR_ROW:] == 3, far, rest) * (1.0 / SCALE)


def spread_tables(lines):
    heads = lines.shape[0]
    constants = [jnp.asarray(v) for v in kinds()]
    lines = lines.reshape(heads // GROUP, GROUP, -1)
    return pl.pallas_call(
        spread_kernel,
        grid=(heads // GROUP,),
        in_specs=[pl.BlockSpec((1,) + lines.shape[1:], lambda g: (g, 0, 0))]
        + [pl.BlockSpec(v.shape, lambda g: (0, 0)) for v in constants],
        out_specs=pl.BlockSpec((GROUP, SLOTS, WIDE), lambda g: (g, 0, 0)),
        out_shape=pltpu.HBM((heads, SLOTS, WIDE), F32),
        compiler_params=params(16),
        cost_estimate=cost(7),
        name="spread_tables",
    )(lines, *constants)


def unskew(tiles, lanes, centre):
    count = lanes // LANES
    wide = tiles[0].shape[1] // LANES
    zero = jnp.zeros((8, LANES), F32)
    total = [zero] * count
    lane = lax.broadcasted_iota(jnp.int32, (8, LANES), 1)
    for t, tile in enumerate(tiles):
        shift = (centre - 8 * t) % lanes
        first, part = shift // LANES, shift % LANES
        pieces = [tile[:, LANES * i : LANES * i + LANES] for i in range(wide)]
        if part:
            pieces = [pltpu.roll(v, part, 1) for v in pieces]
            pieces = [
                jnp.where(lane < part, left, right)
                for left, right in zip([zero] + pieces, pieces + [zero])
            ]
        for i, v in enumerate(pieces):
            total[(first + i) % count] = total[(first + i) % count] + v
    total = jnp.concatenate(total, axis=1)
    row = lax.broadcasted_iota(jnp.int32, (8, lanes), 0)
    out = jnp.where(row == 0, total, 0.0)
    for s in range(1, 8):
        out = out + jnp.where(row == s, pltpu.roll(total, lanes - s, 1), 0.0)
    return jnp.sum(out, axis=0, keepdims=True)


def collect(grad, side, kind_ref, far_kind_ref, spread_ref):
    tiles = FAR_ROW // 8 + 1
    down = OFFSET // 8
    part = jnp.where(kind_ref[: 8 * tiles] == side, grad[: 8 * tiles], 0.0)
    lower = lax.broadcasted_iota(jnp.int32, (8, WIDE), 1) >= TOP
    rows = [part[8 * t : 8 * t + 8] for t in range(tiles)]
    zero = jnp.zeros((8, WIDE), F32)
    both = [
        jnp.where(lower, low, high)
        for high, low in zip(rows + [zero] * down, [zero] * down + rows)
    ]
    far = grad[FAR_ROW:]
    high = far.astype(BF)
    rest = far - high.astype(F32)
    middle = rest.astype(BF)
    low = (rest - middle.astype(F32)).astype(BF)
    count = far.shape[0]
    far = nt(jnp.concatenate([high, middle, low], axis=0), spread_ref[...].astype(BF))
    far = far[:count] + far[count : 2 * count] + far[2 * count :]
    far = jnp.where(far_kind_ref[...] == side, far, 0.0)
    shift = FAR_CENTRE + NEAR - FAR_ROW
    far = [far[8 * t : 8 * t + 8] for t in range(count // 8)]
    return unskew(both, LINE, CENTRE), unskew(far, LANES, shift)


def norm_parts(stream):
    center = stream - jnp.mean(stream, axis=-1, keepdims=True)
    spread = jnp.mean(center * center, axis=-1, keepdims=True)
    rate = lax.rsqrt(spread + 1e-05)
    return center * rate, rate


def norm_back(unit, rate, gain, grad):
    inner = grad * gain
    mean = jnp.mean(inner, axis=-1, keepdims=True)
    along = jnp.mean(inner * unit, axis=-1, keepdims=True)
    return rate * (inner - mean - unit * along)


def tall(v):
    return jnp.concatenate([v, jnp.zeros((WIDE - v.shape[0], v.shape[1]), v.dtype)], axis=0)


def with_ones(v):
    return jnp.concatenate([v.T, jnp.ones((16, v.shape[0]), v.dtype)], axis=0)


def row_sum(v):
    return jnp.sum(v, axis=0, keepdims=True)


def prepare_kernel(core_ref, tokens_ref, cot_ref, x_ref, g_ref):
    images = x_ref.shape[0]
    for i in range(images):
        start = CELLS * i
        low = start // 16 * 16
        keep = lax.broadcasted_iota(jnp.int32, (ROWS, 1), 0) < CELLS
        for ref, out in ((tokens_ref, x_ref), (cot_ref, g_ref)):
            span = min(ROWS + 16, ref.shape[0] - low)
            v = ref[low : low + span].astype(F32)[start - low :]
            if v.shape[0] < ROWS:
                v = jnp.concatenate([v, jnp.zeros((ROWS - v.shape[0], v.shape[1]), F32)], axis=0)
            out[i] = jnp.where(keep, v[:ROWS], 0.0).astype(BF)


def prepare(tokens, cotangent, core):
    rows, width = cotangent.shape
    images = rows // CELLS
    padded = jax.ShapeDtypeStruct((images, ROWS, width), BF)
    whole = lambda shape: pl.BlockSpec(shape, lambda s, core: (0,) * len(shape))
    return pl.pallas_call(
        prepare_kernel,
        grid_spec=pltpu.PrefetchScalarGridSpec(
            num_scalar_prefetch=1,
            grid=(1,),
            in_specs=[
                pl.BlockSpec((rows, width), lambda s, core: (core[0], 0)),
                whole((rows, width)),
            ],
            out_specs=[whole(padded.shape)] * 2,
        ),
        out_shape=[padded] * 2,
        compiler_params=params(24),
        cost_estimate=cost(4),
        name="prepare",
    )(core, tokens, cotangent)


def shard_kernel(input_ref, output_t_ref, expand_t_ref, shrink_ref, out_ref):
    pack = jnp.concatenate([input_ref[t] for t in range(3)] + [output_t_ref[...]], axis=1)
    feed_part = jnp.concatenate([expand_t_ref[...], shrink_ref[...]], axis=1)
    out_ref[...] = jnp.concatenate([pack, feed_part], axis=0).astype(BF)


def shard(input_weight, output_t, expand_t, shrink):
    rows = output_t.shape[0] + shrink.shape[0]
    return pl.pallas_call(
        shard_kernel,
        out_shape=jax.ShapeDtypeStruct((rows, 2 * shrink.shape[1]), BF),
        compiler_params=params(60),
        cost_estimate=cost(1),
        name="shard",
    )(input_weight, output_t, expand_t, shrink)


def update_kernel(grad_ref, *refs):
    half = refs[0].shape[2]
    ins, outs = refs[:8], refs[8:]
    for t in range(3):
        grad = grad_ref[:, half * t : half * t + half]
        new = adamw(ins[0][t], grad, ins[1][t], ins[2][t], ins[3][t], 0.06, 0.05)
        for ref, value in zip(outs[:5], new + (new[0].astype(BF),)):
            ref[t] = value
    grad = grad_ref[:, 3 * half :]
    new = adamw(ins[4][...], grad, ins[5][...], ins[6][...], ins[7][...], 0.3, 0.05)
    for ref, value in zip(outs[5:], new + (new[0].astype(BF),)):
        ref[...] = value


def update(grad, inputs, outputs_t):
    shapes = []
    for v in (inputs[0], outputs_t[0]):
        shapes += [jax.ShapeDtypeStruct(v.shape, F32)] * 4 + [jax.ShapeDtypeStruct(v.shape, BF)]
    return pl.pallas_call(
        update_kernel,
        out_shape=shapes,
        compiler_params=params(16),
        cost_estimate=cost(1),
        name="update",
    )(grad, *inputs, *outputs_t)


def lanes_of(g, size=LANES):
    return pl.ds(pl.multiple_of(g * size, size), size)


def rows_of(g, h, size):
    return pl.ds(pl.multiple_of((g * GROUP + h) * size, size), size)


def place_of(core_ref, a, size):
    away = core_ref[1] ^ a
    out = 0
    for stride, radix in phases(size):
        out = out * radix + ((away >> (stride.bit_length() - 1)) & (radix - 1))
    return out


def assemble(core_ref, near_ref, far_ref, raw_s, win_s, wo_s, wint_ref, wot_ref):
    blocks, rows = near_ref.shape[0], near_ref.shape[1]
    width = wot_ref.shape[0]
    half = width // 2
    core = core_ref[0]
    for a in range(blocks):
        place = place_of(core_ref, a, blocks)
        raw_s[core, rows * a : rows * a + rows] = near_ref[place].astype(F32)
        raw_s[1 - core, rows * a : rows * a + rows] = far_ref[place].astype(F32)
    for t in range(4):
        whole = jnp.concatenate(
            [raw_s[h, :, half * t : half * t + half] for h in range(2)], axis=1
        ).astype(BF)
        if t < 3:
            win_s[:, width * t : width * t + width] = whole
            wint_ref[width * t : width * t + width] = whole.T
        else:
            wot_ref[...] = whole
            wo_s[...] = whole.T


def by_half(top, bottom):
    parts = []
    for g in range(top.shape[1] // LANES):
        lanes = slice(LANES * g, LANES * g + LANES)
        parts += [top[:, lanes], bottom[:, lanes]]
    return jnp.concatenate(parts, axis=1)


def to_slots(mixed, pool):
    high, low = split(mixed)
    far = nn(pool, jnp.concatenate([high, low], axis=0))
    rows = SLOTS - FAR_ROW
    top = jnp.concatenate([mixed[:FAR_ROW], far[:rows]], axis=0).astype(BF)
    bottom = jnp.concatenate([mixed[OFFSET : OFFSET + FAR_ROW], far[rows:]], axis=0).astype(BF)
    width = mixed.shape[1] // 2
    return [by_half(top[:, :width], bottom[:, :width]), by_half(top[:, width:], bottom[:, width:])]


def from_slots(grads, pool_t):
    groups = grads[0].shape[1] // WIDE
    top, bottom = (
        jnp.concatenate(
            [
                grad[:, WIDE * g + LANES * i : WIDE * g + LANES * i + LANES]
                for grad in grads
                for g in range(groups)
            ],
            axis=1,
        )
        for i in range(2)
    )
    high, low = split(jnp.concatenate([top[FAR_ROW:], bottom[FAR_ROW:]], axis=0))
    out = nn(pool_t, jnp.concatenate([high, low], axis=0))
    zeros = lambda count: jnp.zeros((count, top.shape[1]), F32)
    return (
        out
        + jnp.concatenate([top[:FAR_ROW], zeros(ROWS - FAR_ROW)], axis=0)
        + jnp.concatenate(
            [zeros(OFFSET), bottom[:FAR_ROW], zeros(ROWS - FAR_ROW - OFFSET)], axis=0
        )
    )


def turned(slots_ref, target_ref):
    flat = slots_ref[...].T
    for g in range(flat.shape[0] // WIDE):
        for h in range(GROUP):
            for i in range(2):
                source = WIDE * g + LANES * i + HEAD_DIM * h
                target = 2 * HEAD_DIM * (GROUP * g + h) + HEAD_DIM * i
                target_ref[target : target + HEAD_DIM] = flat[source : source + HEAD_DIM]


def masked(source, heads_ref, target_ref):
    for h in range(GROUP):
        target_ref[SLOTS * h : SLOTS * h + SLOTS] = source * heads_ref[h : h + 1]


def sides_of_lanes(v, target_ref):
    lane = lax.broadcasted_iota(jnp.int32, v.shape, 1)
    zero = jnp.zeros_like(v)
    target_ref[:LANES] = jnp.where(lane < TOP, v, zero)
    target_ref[LANES:] = jnp.where(lane < TOP, zero, v)


def choose_half(pair):
    lane = lax.broadcasted_iota(jnp.int32, (HEAD_DIM, WIDE), 1)
    return jnp.where(lane < TOP, pair[:HEAD_DIM], pair[HEAD_DIM:])


HALVES = [slice(0, LANES), slice(LANES, WIDE)]


def forward_kernel(
    core_ref,
    keep_ref,
    near_ref,
    far_ref,
    x_ref,
    vec_ref,
    bias_ref,
    pool_ref,
    heads_ref,
    state_ref,
    att_ref,
    p_ref,
    q_ref,
    k_ref,
    v_ref,
    wint_ref,
    wot_ref,
    raw_s,
    win_s,
    wo_s,
    s_s,
    km_s,
    qb_s,
    vt_s,
    att_t,
    qt_s,
):
    step = pl.program_id(0)
    width = wot_ref.shape[0]
    groups = width // LANES

    @pl.when(step == 0)
    def _():
        assemble(core_ref, near_ref, far_ref, raw_s, win_s, wo_s, wint_ref, wot_ref)

    x = x_ref[...].reshape(PAIR * ROWS, width).astype(F32)
    ln = (norm_parts(x)[0] * vec_ref[0:1] + vec_ref[1:2]).astype(BF)
    mixed = nn(ln, win_s[...])
    for b in range(PAIR):
        own = mixed[ROWS * b : ROWS * b + ROWS]
        query = (own[:, :width] + vec_ref[2:3]).astype(BF)
        q_ref[b] = query
        qt_s[b] = tall(query).T
        shift = jnp.concatenate([jnp.zeros((1, width), F32), vec_ref[3:4]], axis=1)
        k_ref[b], v_ref[b] = to_slots(own[:, width:] + shift, pool_ref[...])
        turned(v_ref.at[b], vt_s.at[b])

    def products(g):
        for b in range(PAIR):
            slot = g % 2 * PAIR + b
            masked(k_ref[b, :, WIDE * g : WIDE * g + WIDE], heads_ref, km_s.at[slot])
            sides_of_lanes(qt_s[b, LANES * g : LANES * g + LANES], qb_s.at[slot])
            s_s[slot] = nn(km_s[slot], qb_s[slot])

    products(0)
    for g in range(groups):
        if g + 1 < groups:
            products(g + 1)
        for b in range(PAIR):
            for h in range(GROUP):
                n = g * GROUP + h
                slots = slice(SLOTS * h, SLOTS * h + SLOTS)
                for half in HALVES:
                    scores = s_s[g % 2 * PAIR + b, slots, half] + bias_ref[n, :, half]
                    top = jnp.max(scores, axis=0, keepdims=True)
                    weights = jnp.exp2((scores - top) * TO_LOG2)
                    total = jnp.sum(weights, axis=0, keepdims=True)
                    p_ref[b, n, :, half] = (weights * (1.0 / total)).astype(BF)
                both = nn(vt_s[b, 2 * HEAD_DIM * n : 2 * HEAD_DIM * (n + 1)], p_ref[b, n])
                att_t[b, HEAD_DIM * n : HEAD_DIM * (n + 1)] = choose_half(both).astype(BF)

    for b in range(PAIR):
        att_ref[b] = att_t[b].T[:ROWS]
    branch = nn(att_ref[...].reshape(PAIR * ROWS, width), wo_s[...]) + vec_ref[4:5]
    for b in range(PAIR):
        scale = DROP_SCALE * keep_ref[step * PAIR + b, 0].astype(F32)
        own = branch[ROWS * b : ROWS * b + ROWS]
        state_ref[b] = x_ref[b].astype(F32) + scale * own


def attend_forward(core, flags, near, far, x, vectors, bias):
    images, _, width = x.shape
    fixed = lambda shape: pl.BlockSpec(shape, lambda s, *_: (0,) * len(shape))
    pair = lambda *shape: pl.BlockSpec((PAIR,) + shape, lambda s, *_: (s,) + (0,) * len(shape))
    pool = np.concatenate([pooling()] * 2, axis=1)
    shapes = [
        ((images, ROWS, width), F32),
        ((images, ROWS, width), BF),
        ((images,) + bias.shape, BF),
        ((images, ROWS, width), BF),
        ((images, SLOTS, 2 * width), BF),
        ((images, SLOTS, 2 * width), BF),
        ((3 * width, width), BF),
        ((width, width), BF),
    ]
    return pl.pallas_call(
        forward_kernel,
        grid_spec=pltpu.PrefetchScalarGridSpec(
            num_scalar_prefetch=2,
            grid=(images // PAIR,),
            in_specs=[
                fixed(near.shape),
                fixed(far.shape),
                pair(ROWS, width),
                fixed(vectors.shape),
                fixed(bias.shape),
                fixed(pool.shape),
                fixed((8, WIDE)),
            ],
            out_specs=[
                pair(ROWS, width),
                pair(ROWS, width),
                pair(*bias.shape),
                pair(ROWS, width),
                pair(SLOTS, 2 * width),
                pair(SLOTS, 2 * width),
                fixed((3 * width, width)),
                fixed((width, width)),
            ],
            scratch_shapes=[
                pltpu.VMEM((2, width, 2 * width), F32),
                pltpu.VMEM((width, 3 * width), BF),
                pltpu.VMEM((width, width), BF),
                pltpu.VMEM((2 * PAIR, GROUP * SLOTS, WIDE), F32),
                pltpu.VMEM((2 * PAIR, GROUP * SLOTS, WIDE), BF),
                pltpu.VMEM((2 * PAIR, WIDE, WIDE), BF),
                pltpu.VMEM((PAIR, 2 * width, SLOTS), BF),
                pltpu.VMEM((PAIR, width, WIDE), BF),
                pltpu.VMEM((PAIR, width, WIDE), BF),
            ],
        ),
        out_shape=[pltpu.HBM(s, d) for s, d in shapes],
        compiler_params=params(60),
        cost_estimate=cost(25),
        name="attend_forward",
    )(
        core,
        flags,
        near,
        far,
        x,
        vectors,
        bias,
        jnp.asarray(pool, BF),
        jnp.asarray(head_rows(), BF),
    )


def feed_kernel(
    core_ref,
    keep_ref,
    state_ref,
    g_ref,
    att_ref,
    ff0_ref,
    ff1_ref,
    wot_ref,
    vec_ref,
    fb_ref,
    result_ref,
    grad_ref,
    dout_ref,
    dff0_ref,
    dff1_ref,
    dwot_ref,
    rows_ref,
    ws_s,
    we_s,
    ff0_s,
    ff1_s,
):
    step = pl.program_id(0)
    last = pl.num_programs(0) - 1
    width = wot_ref.shape[0]
    chunks = 2 * dff0_ref.shape[0] // width
    blocks, block = ff0_ref.shape[0], ff0_ref.shape[1]
    count = MANY * ROWS

    @pl.when(step == 0)
    def _():
        ws_s[...] = jnp.zeros_like(ws_s)
        we_s[...] = jnp.zeros_like(we_s)
        dwot_ref[...] = jnp.zeros_like(dwot_ref)
        rows_ref[...] = jnp.zeros_like(rows_ref)
        for a in range(blocks):
            place = place_of(core_ref, a, blocks)
            here = slice(block * a, block * a + block)
            ff0_s[here] = ff0_ref[place]
            ff1_s[here] = ff1_ref[place]

    def column(which):
        row = lax.broadcasted_iota(jnp.int32, (count, 1), 0)
        out = keep_ref[step * MANY, which].astype(F32)
        for b in range(1, MANY):
            out = jnp.where(row < b * ROWS, out, keep_ref[step * MANY + b, which].astype(F32))
        return jnp.broadcast_to(out * DROP_SCALE, (count, 1))

    state = state_ref[...].reshape(count, width)
    upstream = g_ref[...].reshape(count, width).astype(F32)
    unit, rate = norm_parts(state)
    gain = vec_ref[5:6]
    ln = (unit * gain + vec_ref[6:7]).astype(BF)
    keep = column(1)
    scaled = keep * upstream
    signal = scaled.astype(BF)
    ln_t = with_ones(ln)
    signal_t = signal.T

    out = jnp.zeros((count, width), F32)
    grad_ln = jnp.zeros((count, width), F32)
    for c in range(chunks):
        piece = slice(width * c, width * c + width)
        ff_s = ff0_s if c < chunks // 2 else ff1_s
        here = slice(width * (c % (chunks // 2)), width * (c % (chunks // 2)) + width)
        we, ws = ff_s[here, :width], ff_s[here, width:]
        row = (c + core_ref[0] * (chunks // 2)) % chunks
        pre = nt(ln, we) + fb_ref[pl.ds(row, 1)]
        part = 0.5 * (1.0 + lax.erf(pre * np.float32(0.5**0.5)))
        act = (pre * part).astype(BF)
        slope = part + pre * (jnp.exp(-0.5 * pre * pre) * np.float32((2 * np.pi) ** -0.5))
        grad_pre = (nt(signal, ws) * slope).astype(BF)
        out = out + nn(act, ws)
        grad_ln = grad_ln + nn(grad_pre, we)
        ws_s[:, piece] += nn(signal_t, act)
        part = nn(ln_t, grad_pre)
        we_s[:, piece] += part[:width]
        rows_ref[pl.ds(4 + row, 1)] += part[width : width + 1]

    result = state + keep * (out + vec_ref[7:8])
    grad_state = upstream + norm_back(unit, rate, gain, grad_ln)
    for b in range(MANY):
        result_ref[CELLS * b : CELLS * b + CELLS] = result[ROWS * b : ROWS * b + CELLS]
    grad_ref[...] = grad_state.reshape(MANY, ROWS, width)
    scaled_one = column(0) * grad_state
    one = scaled_one.astype(BF)
    dout_ref[...] = nn(one, wot_ref[...]).astype(BF).reshape(MANY, ROWS, width)
    dwot_ref[...] += nn(one.T, att_ref[...].reshape(count, width))
    rows_ref[0:1] += row_sum(scaled_one)
    rows_ref[1:2] += row_sum(grad_ln * unit)
    rows_ref[2:3] += row_sum(grad_ln)
    rows_ref[3:4] += row_sum(scaled)

    @pl.when(step == last)
    def _():
        half = chunks // 2
        for c in range(chunks):
            piece = slice(width * c, width * c + width)
            here = slice(width * (c % half), width * (c % half) + width)
            target = dff0_ref if c < half else dff1_ref
            target[here, :width] = we_s[:, piece].astype(BF).T
            target[here, width:] = ws_s[:, piece].astype(BF).T


def feed(core, flags, state, g, att, ff0, ff1, wot, vectors, fb):
    images, _, width = state.shape
    hidden = 2 * ff0.shape[0] * ff0.shape[1]
    fixed = lambda shape: pl.BlockSpec(shape, lambda s, *_: (0,) * len(shape))
    pair = lambda *shape: pl.BlockSpec((MANY,) + shape, lambda s, *_: (s,) + (0,) * len(shape))
    shapes = [
        ((images * CELLS, width), F32),
        ((images, ROWS, width), F32),
        ((images, ROWS, width), BF),
        ((hidden // 2, 2 * width), BF),
        ((hidden // 2, 2 * width), BF),
        ((width, width), F32),
        ((8, width), F32),
    ]
    return pl.pallas_call(
        feed_kernel,
        grid_spec=pltpu.PrefetchScalarGridSpec(
            num_scalar_prefetch=2,
            grid=(images // MANY,),
            in_specs=[
                pair(ROWS, width),
                pair(ROWS, width),
                pair(ROWS, width),
                fixed(ff0.shape),
                fixed(ff1.shape),
                fixed((width, width)),
                fixed(vectors.shape),
                fixed(fb.shape),
            ],
            out_specs=[
                pl.BlockSpec((MANY * CELLS, width), lambda s, *_: (s, 0)),
                pair(ROWS, width),
                pair(ROWS, width),
                fixed((hidden // 2, 2 * width)),
                fixed((hidden // 2, 2 * width)),
                fixed((width, width)),
                fixed((8, width)),
            ],
            scratch_shapes=[
                pltpu.VMEM((width, hidden), F32),
                pltpu.VMEM((width, hidden), F32),
                pltpu.VMEM((hidden // 2, 2 * width), BF),
                pltpu.VMEM((hidden // 2, 2 * width), BF),
            ],
        ),
        out_shape=[jax.ShapeDtypeStruct(s, d) for s, d in shapes],
        compiler_params=params(56),
        cost_estimate=cost(35),
        name="feed",
    )(core, flags, state, g, att, ff0, ff1, wot, vectors, fb)


def add_kernel(one_ref, two_ref, out_ref):
    out_ref[...] = one_ref[...] + two_ref[...]


def add(one, two):
    rows, lanes = one.shape
    block = pl.BlockSpec((rows // 2, lanes), lambda s: (s, 0))
    return pl.pallas_call(
        add_kernel,
        grid=(2,),
        in_specs=[block, block],
        out_specs=block,
        out_shape=jax.ShapeDtypeStruct(one.shape, one.dtype),
        compiler_params=params(16),
        cost_estimate=cost(1.5),
        name="add",
    )(one, two)


def diagonal(whole):
    lane = lax.broadcasted_iota(jnp.int32, (SLOTS, WIDE), 1) % LANES
    out = whole[SLOTS * (GROUP - 1) :]
    for h in reversed(range(GROUP - 1)):
        out = jnp.where(lane < HEAD_DIM * (h + 1), whole[SLOTS * h : SLOTS * h + SLOTS], out)
    return out


def sides_of_rows(v, target_ref):
    row = lax.broadcasted_iota(jnp.int32, v.shape, 0)
    zero = jnp.zeros_like(v)
    target_ref[:, :LANES] = jnp.where(row < TOP, v, zero)
    target_ref[:, LANES:] = jnp.where(row < TOP, zero, v)


def small_rows(lines_ref, vector_rows, core):
    groups = lines_ref.shape[0]
    heads = groups * GROUP
    lanes = 2 * LINE
    first, rest = [], []
    for i in range(heads):
        g, h = i // GROUP, i % GROUP
        pair = [lines_ref[g, side, h : h + 1] for side in range(2)]
        first.append(jnp.concatenate([v[:, :LINE] for v in pair], axis=1))
        rest += [v[:, LINE:] for v in pair]
    per_row = lanes // LANES
    rest = [jnp.concatenate(rest[i : i + per_row], axis=1) for i in range(0, len(rest), per_row)]
    sums = [
        jnp.concatenate([vector_rows[i : i + 1], vector_rows[i + 1 : i + 2]], axis=1)
        for i in range(0, vector_rows.shape[0], 2)
    ]
    halves = [
        jnp.concatenate(
            [
                row
                for rows in (first, rest, sums)
                for row in rows[len(rows) // 2 * c : len(rows) // 2 * (c + 1)]
            ],
            axis=0,
        )
        for c in range(2)
    ]
    return jnp.where(core == 0, halves[0], halves[1])


def backward_kernel(
    core_ref,
    x_ref,
    grad_ref,
    dout_ref,
    q_ref,
    k_ref,
    v_ref,
    p_ref,
    wint_ref,
    vec_ref,
    dwot_ref,
    rows_two_ref,
    pool_t_ref,
    heads_ref,
    kind_ref,
    far_kind_ref,
    spread_ref,
    igrad_ref,
    near_ref,
    far_ref,
    dwin_s,
    rows_s,
    lines_s,
    dense0_s,
    dense1_s,
    dense2_s,
    dense3_s,
    k_t,
    raw_qt,
    raw_k,
    raw_v,
    mixed_s,
    whole_s,
    d_s,
    ds_s,
    vm_s,
    db_s,
    qr_s,
    dr_s,
):
    phase, step = pl.program_id(0), pl.program_id(1)
    width = wint_ref.shape[1]
    groups = width // LANES
    now, before = phase % 2, (phase + 1) % 2
    dense_refs = (dense0_s, dense1_s, dense2_s, dense3_s)

    def collect_before():
        g = jnp.maximum(phase - 1, 0)
        for h in range(GROUP):
            fine, far = collect(
                dense_refs[h][before], step + 1, kind_ref, far_kind_ref, spread_ref
            )
            lines_s[g, step, h : h + 1, :LINE] = fine
            lines_s[g, step, h : h + 1, LINE:] = far

    @pl.when((phase == 0) & (step == 0))
    def _():
        dwin_s[...] = jnp.zeros_like(dwin_s)
        rows_s[...] = jnp.zeros_like(rows_s)
        for ref in dense_refs:
            ref[...] = jnp.zeros_like(ref)

    @pl.when((phase > 0) & (phase < groups) & (step == 0))
    def _():
        for ref in dense_refs:
            ref[now] = jnp.zeros(ref.shape[1:], F32)

    @pl.when((phase > 0) & (phase < groups))
    def _():
        collect_before()

    @pl.when(phase < groups)
    def _():
        def products(i):
            for b in range(PAIR):
                n = i * PAIR + b
                keys, values = k_ref[n], v_ref[n]
                flat = keys.T
                for h in range(GROUP):
                    for side in range(2):
                        source = LANES * side + HEAD_DIM * h
                        target = HEAD_DIM * (2 * h + side)
                        k_t[i * PAIR + b, target : target + HEAD_DIM] = flat[source : source + HEAD_DIM]
                masked(values, heads_ref, vm_s.at[i * PAIR + b])
                dout = tall(dout_ref[n])
                sides_of_lanes(dout.T, db_s.at[i * PAIR + b])
                d_s[i * PAIR + b] = nn(vm_s[i * PAIR + b], db_s[i * PAIR + b])
                sides_of_rows(tall(q_ref[n]), qr_s.at[i * PAIR + b])
                sides_of_rows(dout, dr_s.at[i * PAIR + b])

        def attend(i):
            for h in range(GROUP):
                slots = slice(SLOTS * h, SLOTS * h + SLOTS)
                for half in HALVES:
                    dense = dense_refs[h][now, :, half]
                    for b in range(PAIR):
                        probs = p_ref[i * PAIR + b, h, :, half].astype(F32)
                        grad_probs = d_s[i * PAIR + b, slots, half]
                        along = jnp.sum(probs * grad_probs, axis=0, keepdims=True)
                        grad_scores = (probs * (grad_probs - along)).astype(BF)
                        ds_s[i * PAIR + b, slots, half] = grad_scores
                        dense = dense + grad_scores.astype(F32)
                    dense_refs[h][now, :, half] = dense
                for b in range(PAIR):
                    both = nn(k_t[i * PAIR + b, 2 * HEAD_DIM * h : 2 * HEAD_DIM * (h + 1)], ds_s[i * PAIR + b, slots])
                    raw_qt[step * MANY + i * PAIR + b, rows_of(phase, h, HEAD_DIM), :] = (
                        choose_half(both) * SCALE
                    ).astype(BF)
            wide = lanes_of(phase, WIDE)
            for b in range(PAIR):
                n = step * MANY + i * PAIR + b
                probs = p_ref[i * PAIR + b].reshape(GROUP * SLOTS, WIDE)
                raw_v[n, :, wide] = diagonal(nn(probs, dr_s[i * PAIR + b]))
                raw_k[n, :, wide] = diagonal(nn(ds_s[i * PAIR + b], qr_s[i * PAIR + b])) * SCALE

        products(0)
        for i in range(MANY // PAIR):
            if i + 1 < MANY // PAIR:
                products(i + 1)
            attend(i)

    @pl.when(phase == groups)
    def _():
        collect_before()
        gain = vec_ref[0:1]
        for i in range(MANY // PAIR):
            for b in range(PAIR):
                n = step * MANY + i * PAIR + b
                rows = slice(ROWS * b, ROWS * b + ROWS)
                mixed_s[rows, :width] = raw_qt[n].T[:ROWS]
                mixed_s[rows, width:] = from_slots([raw_k[n], raw_v[n]], pool_t_ref[...]).astype(BF)
            mixed = mixed_s[...]
            own = slice(PAIR * i, PAIR * i + PAIR)
            x = x_ref[own].reshape(PAIR * ROWS, width).astype(F32)
            unit, rate = norm_parts(x)
            ln = (unit * gain + vec_ref[1:2]).astype(BF)
            part = nn(with_ones(ln), mixed)
            dwin_s[...] += part[:width]
            sums = part[width:]
            grad_ln = nn(mixed, wint_ref[...])
            out = grad_ref[own].reshape(PAIR * ROWS, width) + norm_back(unit, rate, gain, grad_ln)
            for b in range(PAIR):
                n = PAIR * i + b
                igrad_ref[CELLS * n : CELLS * n + CELLS] = out[ROWS * b : ROWS * b + CELLS]
            rows_s[0:1] += row_sum(grad_ln * unit)
            rows_s[1:2] += row_sum(grad_ln)
            rows_s[2:3] += sums[:1, :width]
            rows_s[3:4] += sums[:1, 2 * width :]

    @pl.when((phase == groups) & (step == pl.num_programs(1) - 1))
    def _():
        rows = near_ref.shape[1]
        blocks = width // rows
        half = width // 2
        core = core_ref[0]
        for h in range(2):
            parts = [
                dwin_s[:, width * t + half * h : width * t + half * h + half] for t in range(3)
            ] + [dwot_ref[:, half * h : half * h + half]]
            whole_s[h] = jnp.concatenate(parts, axis=1)
        for a in range(blocks):
            place = place_of(core_ref, a, blocks)
            here = slice(rows * a, rows * a + rows)
            near_ref[place] = whole_s[core, here].astype(BF)
            far_ref[place] = whole_s[1 - core, here].astype(BF)
        sums = jnp.concatenate([rows_s[:4], rows_two_ref[...]], axis=0)
        extra = near_ref.shape[0] - blocks
        for ref, which in ((near_ref, core), (far_ref, 1 - core)):
            small = small_rows(lines_s, sums, which)
            pad = jnp.zeros((extra * rows - small.shape[0], small.shape[1]), F32)
            small = jnp.concatenate([small, pad], axis=0) if pad.shape[0] else small
            for i in range(extra):
                ref[blocks + i] = small[rows * i : rows * i + rows].astype(BF)


SMALL = 11


def attend_backward(
    core, pack_shape, x, grad, dout, q, k, v, probs, win_t, vectors, dwot, rows_two
):
    images, _, width = x.shape
    groups = width // LANES
    end = images // MANY - 1
    fixed = lambda shape: pl.BlockSpec(shape, lambda p, s, *_: (0,) * len(shape))
    late = lambda *shape: pl.BlockSpec(
        (MANY,) + shape,
        lambda p, s, *_: (jnp.where(p == groups, s, 0),) + (0,) * len(shape),
    )

    def early(shape, axis):
        def where(p, s, *_):
            place = [jnp.where(p == groups, end, s)] + [0] * len(shape)
            place[axis] = jnp.minimum(p, groups - 1)
            return tuple(place)

        return pl.BlockSpec((MANY,) + shape, where)

    blocks, rows, lanes = pack_shape
    pack_shape = (blocks + -(-SMALL // rows), rows, lanes)
    pool_t = np.concatenate([pooling().T] * 2, axis=1)
    tables = kinds()
    shapes = [((images * CELLS, width), F32), (pack_shape, BF), (pack_shape, BF)]
    stack = (MANY, GROUP * SLOTS, WIDE)
    square = (MANY, WIDE, WIDE)
    return pl.pallas_call(
        backward_kernel,
        grid_spec=pltpu.PrefetchScalarGridSpec(
            num_scalar_prefetch=1,
            grid=(groups + 1, images // MANY),
            in_specs=[
                late(ROWS, width),
                late(ROWS, width),
                early((ROWS, LANES), 2),
                early((ROWS, LANES), 2),
                early((SLOTS, WIDE), 2),
                early((SLOTS, WIDE), 2),
                early((GROUP, SLOTS, WIDE), 1),
                fixed(win_t.shape),
                fixed(vectors.shape),
                fixed(dwot.shape),
                fixed(rows_two.shape),
                fixed(pool_t.shape),
                fixed((8, WIDE)),
            ]
            + [fixed(v.shape) for v in tables],
            out_specs=[
                pl.BlockSpec(
                    (MANY * CELLS, width), lambda p, s, *_: (jnp.where(p == groups, s, 0), 0)
                ),
                fixed(pack_shape),
                fixed(pack_shape),
            ],
            scratch_shapes=[
                pltpu.VMEM((width, 3 * width), F32),
                pltpu.VMEM((8, width), F32),
                pltpu.VMEM((groups, 2, GROUP, LINE + LANES), F32),
                pltpu.VMEM((2, SLOTS, WIDE), F32),
                pltpu.VMEM((2, SLOTS, WIDE), F32),
                pltpu.VMEM((2, SLOTS, WIDE), F32),
                pltpu.VMEM((2, SLOTS, WIDE), F32),
                pltpu.VMEM((MANY, WIDE, SLOTS), BF),
                pltpu.VMEM((images, width, WIDE), BF),
                pltpu.VMEM((images, SLOTS, 2 * width), F32),
                pltpu.VMEM((images, SLOTS, 2 * width), F32),
                pltpu.VMEM((PAIR * ROWS, 3 * width), BF),
                pltpu.VMEM((2, width, 2 * width), F32),
                pltpu.VMEM(stack, F32),
                pltpu.VMEM(stack, BF),
                pltpu.VMEM(stack, BF),
                pltpu.VMEM(square, BF),
                pltpu.VMEM(square, BF),
                pltpu.VMEM(square, BF),
            ],
        ),
        out_shape=[jax.ShapeDtypeStruct(s, d) for s, d in shapes],
        compiler_params=params(60),
        cost_estimate=cost(45),
        name="attend_backward",
    )(
        core,
        x,
        grad,
        dout,
        q,
        k,
        v,
        probs,
        win_t,
        vectors,
        dwot,
        rows_two,
        jnp.asarray(pool_t, BF),
        jnp.asarray(head_rows(), BF),
        *[jnp.asarray(v) for v in tables],
    )


def phases(size):
    out, stride = [], 1
    while stride < size:
        radix = 4 if size // stride % 4 == 0 else 2
        out.append((stride, radix))
        stride *= radix
    return out


def hop(v, stride, mask):
    return lax.ppermute(
        v, "dp", [(i, i ^ (mask * stride)) for i in range(lax.axis_size("dp"))]
    )


def meet(v, stride, radix):
    return jnp.stack([v] + [hop(v, stride, m) for m in range(1, radix)])


def swap(v):
    return lax.ppermute(v, "head", [(0, 1), (1, 0)])


def exchange(v):
    return lax.all_to_all(v, "dp", 0, 0)


def repeat(v, times):
    return jnp.broadcast_to(v[None], (times,) + v.shape)


def tree_sum(parts):
    while len(parts) > 1:
        parts = [parts[i] + parts[i + 1] for i in range(0, len(parts), 2)]
    return parts[0]


def reduce_parts(v, small):
    blocks, rows, lanes = v.shape
    v = v.reshape(blocks * rows, lanes)
    for stride, radix in phases(blocks):
        count = v.shape[0] // radix
        small = small.astype(BF)
        got = [
            hop(
                jnp.concatenate([v[count * m : count * m + count].astype(BF), small], axis=0),
                stride,
                m,
            ).astype(F32)
            for m in range(1, radix)
        ]
        v = tree_sum([v[:count]] + [g[:count] for g in got])
        small = tree_sum([small.astype(F32)] + [g[count:] for g in got])
    return v, small


def by_core(core, near, far):
    return jnp.where(core == 0, near, far), jnp.where(core == 0, far, near)


def adamw(weight, grad, first, second, average, rate, decay):
    first = 0.9 * first + 0.1 * grad
    second = 0.999 * second + 0.001 * grad * grad
    fix_one = 1.0 - 0.9**STEP
    fix_two = 1.0 - 0.999**STEP
    weight = weight - rate * (
        first / fix_one / (jnp.sqrt(second / fix_two) + 1e-08) + decay * weight
    )
    average = 0.9 * average + 0.1 * weight
    return (weight, first, second, average)


def shards(
    tokens,
    keep,
    cotangent,
    input_weight,
    output_weight,
    expand_weight,
    shrink_weight,
    bias_tables,
    vectors,
    first_input,
    second_input,
    average_input,
    first_output,
    second_output,
    average_output,
    first_expand,
    second_expand,
    average_expand,
    first_shrink,
    second_shrink,
    average_shrink,
    first_tables,
    second_tables,
    average_tables,
    first_vectors,
    second_vectors,
    average_vectors,
):
    dp, head = lax.axis_size("dp"), lax.axis_size("head")
    core = lax.axis_index("head")
    width = vectors.shape[1]
    own_images = cotangent.shape[0] // CELLS
    rows = input_weight.shape[1]
    hidden = expand_weight.shape[1] * dp * head
    block = hidden // (dp * head)

    part = shard(input_weight, output_weight.T, expand_weight.T, shrink_weight)
    pick = jnp.stack([core, lax.axis_index("dp")]).astype(jnp.int32)
    tables = by_core(core, bias_tables, swap(bias_tables))
    lines = table_lines(jnp.concatenate(tables, axis=0))
    x, g = prepare(tokens, cotangent, pick)
    *high, low = reversed(phases(dp))
    for stride, radix in high:
        part = meet(part, stride, radix)
    lines, part, x, g = lax.optimization_barrier((lines, part, x, g))
    bias = spread_tables(lines)
    part = part.reshape(-1, *part.shape[-2:])
    pack0 = meet(part[:, :rows], *low)
    ff, pack0, bias = lax.optimization_barrier((part[:, rows:], pack0, bias))
    pack0 = pack0.reshape(dp, rows, 2 * width)
    pack1 = swap(pack0)
    ff_parts = [ff] + [hop(ff, low[0], m) for m in range(1, low[1])]
    flags = lax.dynamic_slice_in_dim(keep, core * own_images, own_images, 0)
    fb = vectors[8:].reshape(dp, head, block).swapaxes(0, 1).reshape(-1, width)

    state, att, probs, q, k, v, win_t, wot = attend_forward(
        pick, flags, pack0, pack1, x, vectors, bias
    )
    ff_parts, state = lax.optimization_barrier((ff_parts, state))
    ff0 = jnp.concatenate(ff_parts, axis=0)
    ff1 = swap(ff0)
    result, grad_state, dout, dff0, dff1, dwot, rows_two = feed(
        pick, flags, state, g, att, ff0, ff1, wot, vectors, fb
    )
    dff = add(dff0, swap(dff1)).reshape(dp, block, 2 * width)
    dff, dout = lax.optimization_barrier((dff, dout))
    dff = exchange(dff)
    input_grad, dpack0, dpack1 = attend_backward(
        pick,
        pack0.shape,
        x,
        grad_state,
        dout,
        q,
        k,
        v,
        probs,
        win_t,
        vectors,
        dwot,
        rows_two,
    )
    dff, dpack1 = lax.optimization_barrier((dff, dpack1))
    ff_grad = jnp.sum(dff.astype(F32), axis=0)

    dpack = dpack0.astype(F32) + swap(dpack1).astype(F32)
    small = dpack[dp:].reshape(-1, 2 * width)[: -(-SMALL // 8) * 8]
    pack_grad, small = reduce_parts(dpack[:dp], small)
    local_heads = bias_tables.shape[0]
    lines = small[:local_heads]
    far = small[local_heads : local_heads + local_heads // 3].reshape(local_heads, 2, LANES)
    table_grad = table_from_lines(lines[:, :LINE], lines[:, LINE:], far[:, 0], far[:, 1])
    own_vector = small[local_heads + local_heads // 3 : SMALL]
    vector_total = jnp.concatenate(by_core(core, own_vector, swap(own_vector)))
    vector_total = vector_total.reshape(vectors.shape)
    fb_total = vector_total[8:].reshape(head, dp, block).swapaxes(0, 1).reshape(-1, width)
    vector_total = jnp.concatenate([vector_total[:8], fb_total])

    new = update(
        pack_grad,
        (input_weight, first_input, second_input, average_input),
        (output_weight.T, first_output.T, second_output.T, average_output.T),
    )
    input_new, output_new = new[:5], [v.T for v in new[5:]]
    grad_expand = ff_grad[:, :width].T
    grad_shrink = ff_grad[:, width:]
    expand_new = adamw(
        expand_weight, grad_expand, first_expand, second_expand, average_expand, 0.06, 0.05
    )
    shrink_new = adamw(
        shrink_weight, grad_shrink, first_shrink, second_shrink, average_shrink, 0.06, 0.05
    )
    tables_new = adamw(
        bias_tables, table_grad, first_tables, second_tables, average_tables, 1.0, 0.0
    )
    vectors_new = adamw(
        vectors, vector_total, first_vectors, second_vectors, average_vectors, 0.6, 0.0
    )
    return (
        result,
        input_grad,
        *input_new,
        *output_new,
        *expand_new,
        expand_new[0].astype(BF),
        *shrink_new,
        shrink_new[0].astype(BF),
        *tables_new,
        *vectors_new,
    )


def solution(mesh):
    both = P(("dp", "head"), None)
    inputs = P(None, "dp", "head")
    output = P("head", "dp")
    expand = P(None, ("dp", "head"))
    tables = P("head", None)
    in_specs = (
        (P("dp", None), P("dp", None), both, inputs, output, expand, both, tables, P())
        + (inputs,) * 3
        + (output,) * 3
        + (expand,) * 3
        + (both,) * 3
        + (tables,) * 3
        + (P(),) * 3
    )
    out_specs = (
        (both, both)
        + (inputs,) * 5
        + (output,) * 5
        + (expand,) * 5
        + (both,) * 5
        + (tables,) * 4
        + (P(),) * 4
    )
    return jax.shard_map(shards, mesh=mesh, in_specs=in_specs, out_specs=out_specs, check_vma=False)
```

time: 1520 us -> 164 us (0.11)
  local copies, waits for them, and re-layouts: 552 us -> 14.1 us
  other arithmetic: 450 us -> 5.24 us
  waiting for transfers between devices: 221 us -> 20.1 us
  matrix products: 154 us -> 0 us
  blocking collectives: 110 us -> 0 us
  Pallas kernels: 0 us -> 92.7 us
  starting transfers between devices: 0.55 us -> 30.1 us
  between operations: 17.9 us -> 1.58 us
    scatter-add x1 -> x0, other arithmetic: 230 us -> none  [attend(): bias = jnp.transpose(table[:, index], (1, 0, 2, 3))]
    dot_general x18 -> x0, matrix products: 154 us -> none  [the longest x6 59.2 us: product_plain(): jnp.einsum(form, left.astype(jnp.bfloat16), right.astype(jnp.bfloat16), p...]
    convert_element_type x13 -> x1, local copies, waits for them, and re-layouts: 116 us -> 0.01 us  [reduce_parts(): small = small.astype(BF)]
    reduce_scatter x5 -> x0, waiting for transfers between devices: 112 us -> none  [the longest x1 95.8 us: shards(): lax.psum_scatter(grad_shrink, ('dp', 'head'), scatter_dimension=0, tiled=...]
    reduce_sum x16 -> x1, other arithmetic: 110 us -> 0.16 us  [shards(): ff_grad = jnp.sum(dff.astype(F32), axis=0)]
    all_gather x3 -> x0, waiting for transfers between devices: 109 us -> none  [the longest x1 56.9 us: shards(): lax.all_gather(shrink_weight.astype(jnp.bfloat16), ('dp', 'head'), axis=0...]
    gather x3 -> x0, local copies, waits for them, and re-layouts: 103 us -> none  [attend(): bias = jnp.transpose(table[:, index], (1, 0, 2, 3))]
    another operation x10 -> x1, local copies, waits for them, and re-layouts: 94.7 us -> 0.02 us  [meet(): return jnp.stack([v] + [hop(v, stride, m) for m in range(1, radix)])]
  transfers between devices with their start and end apart: 9 -> 22, of which waited for: 5 -> 9; matrix products, arithmetic and copies ran while one was open for 46% -> 5% of each run, Pallas kernels for 0% -> 35%
where the time goes in v1:
time: 164 us
  Pallas kernels  92.7 us (57%)
  starting transfers between devices  30.1 us (18%)
  waiting for transfers between devices  20.1 us (12%)
  local copies, waits for them, and re-layouts  14.1 us (9%)
  other arithmetic  5.24 us (3%)
    pallas_call x1, Pallas kernels, feed(): pl.pallas_call(feed_kernel, grid_spec=pltpu.PrefetchScalarGridSpec(num_sc...  31.6 us
    pallas_call x1, Pallas kernels, attend_backward(): pl.pallas_call(backward_kernel, grid_spec=pltpu.PrefetchScalarGridSpec(nu...  30.9 us
    pallas_call x1, Pallas kernels, attend_forward(): pl.pallas_call(forward_kernel, grid_spec=pltpu.PrefetchScalarGridSpec(num...  21.3 us
    ppermute x15, starting transfers between devices, hop(): lax.ppermute(v, 'dp', [(i, i ^ mask * stride) for i in range(lax.axis_siz...  16.4 us
    ppermute x15, waiting for transfers between devices, hop(): lax.ppermute(v, 'dp', [(i, i ^ mask * stride) for i in range(lax.axis_siz...  15.3 us
    unnamed x88, local copies, waits for them, and re-layouts  9.86 us
    ppermute x6, starting transfers between devices, swap(): return lax.ppermute(v, 'head', [(0, 1), (1, 0)])  8.76 us
    all_to_all x1, starting transfers between devices, exchange(): return lax.all_to_all(v, 'dp', 0, 0)  4.98 us
  transfers between devices with their start and end apart: 22, of which 9 were waited for; matrix products, arithmetic and copies ran while one was open for 5% of the time, Pallas kernels for 35%

profile of v1, /device:TPU:1, one launch (start us, length us, event | category | flops | bytes accessed | tf_op | source)
XLA Modules:
  0.0 163.8 jit_solution(16454186280802932847)
XLA Ops:
  0.7 1.8 %shard.1 = bf16[72,768]{1,0:T(8,128)(2,1)} custom-call(f32[3,24,192]{2,1,0:T(8,128)} %refs_0_.1, f32[24,192]{1,0:T(8,128)} %bitcast.54, f32[48,384]{1,0:T(8,128)} %bitcast.74, f32[48,384]{1,0:T(8,128)} %shrink_ref.1), custom_call_target="tpu_custom_call" | custom-call | flops 1150000000 | tf_op jit(solution)/shard_map/shard/pallas_call | solution.py:318
  2.6 4.2 %collective-permute-start.3 = (bf16[72,768]{1,0:T(8,128)(2,1)}, bf16[72,768]{1,0:T(8,128)(2,1)S(1)}, u32[]{:S(2)}, u32[]{:S(2)}) collective-permute-start(bf16[72,768]{1,0:T(8,128)(2,1)} %shard.1), channel_id=1, source_target_pairs={{0,24},{2,26},{4,28},{6,30},{8,16},{10,18},{12,20},{14,22},{16,8},... | collective-permute-start | bytes 331784 | tf_op jit(solution)/shard_map/ppermute | solution.py:1123
  7.0 1.2 collective-permute-start
  8.3 1.3 copy-done.2
  9.6 0.9 prepare.1
  10.5 1.1 copy-done.16
  11.6 1.2 copy-done.17
  14.5 1.3 collective-permute-done.2
  15.9 1.3 collective-permute-start.5
  17.2 1.2 collective-permute-start.4
  18.7 4.2 %spread_tables.1.bias_ref = f32[12,192,256]{2,1,0:T(8,128)} custom-call(f32[3,4,1024]{2,1,0:T(4,128)S(1)} %reshape.141.line_ref, s32[192,256]{1,0:T(8,128)S(1)} %copy-done.11, s32[56,128]{1,0:T(8,128)S(1)} %copy-done.13, f32[128,256]{1,0:T(8,128)S(1)} %copy-done.12), custom_call_target="tpu_custom_call" | custom-call | flops 8049999872 | tf_op jit(solution)/shard_map/spread_tables/pallas_call | solution.py:183
  22.9 2.3 %collective-permute-done.6 = bf16[4,24,768]{2,1,0:T(8,128)(2,1)S(1)} collective-permute-done((bf16[4,24,768]{2,1,0:T(8,128)(2,1)S(1)}, bf16[4,24,768]{2,1,0:T(8,128)(2,1)S(1)}, u32[]{:S(2)}, u32[]{:S(2)}) %collective-permute-start.6) | collective-permute-done | bytes 147488 | tf_op jit(solution)/shard_map/ppermute | solution.py:1123
  25.3 2.0 %collective-permute-start.10 = (bf16[16,24,768]{2,1,0:T(8,128)(2,1)S(1)}, bf16[16,24,768]{2,1,0:T(8,128)(2,1)S(1)}, u32[]{:S(2)}, u32[]{:S(2)}) collective-permute-start(bf16[16,24,768]{2,1,0:T(8,128)(2,1)S(1)} %bitcast.61), channel_id=1, source_target_pairs={{0,1},{1,0},{2,3},{3,2},{4,5},{5,4},{6,7},{7,6},{8,9},{9,8},{10,11... | collective-permute-start | bytes 1769480 | tf_op jit(solution)/shard_map/ppermute | solution.py:1133
  27.4 0.7 copy.79.keep_ref
  28.0 1.6 %collective-permute-start.9 = (bf16[4,48,768]{2,1,0:T(8,128)(2,1)S(1)}, bf16[4,48,768]{2,1,0:T(8,128)(2,1)S(1)}, u32[]{:S(2)}, u32[]{:S(2)}) collective-permute-start(bf16[4,48,768]{2,1,0:T(8,128)(2,1)S(1)} %slice.182), channel_id=1, source_target_pairs={{0,6},{2,4},{4,2},{6,0},{8,14},{10,12},{12,10},{14,8},{16,22},{18,... | collective-permute-start | bytes 884744 | tf_op jit(solution)/shard_map/ppermute | solution.py:1123
  29.9 0.8 collective-permute-start.7
  30.7 0.8 copy-done.40
  31.5 21.3 %attend_forward.1 = (f32[8,208,384]{2,1,0:T(8,128)}, bf16[8,208,384]{2,1,0:T(8,128)(2,1)}, bf16[8,12,192,256]{3,2,1,0:T(8,128)(2,1)}, bf16[8,208,384]{2,1,0:T(8,...) custom-call(s32[2]{0:T(128)} %copy-done.14, ...), custom_call_target="tpu_custom_call" | custom-call | flops 28750000128 | tf_op jit(solution)/shard_map/attend_forward/pallas_call | solution.py:560
  52.9 0.7 constant_dynamic-update-slice_fusion.3
  53.6 0.7 constant_dynamic-update-slice_fusion.2
  54.3 0.7 constant_dynamic-update-slice_fusion.1
  55.1 0.7 constant_dynamic-update-slice_fusion.ff0_ref
  55.8 0.9 collective-permute-start.11
  56.8 0.7 reshape.144.fb_ref
  57.5 1.9 %collective-permute-done.11.ff1_ref = bf16[16,48,768]{2,1,0:T(8,128)(2,1)S(1)} collective-permute-done((bf16[16,48,768]{2,1,0:T(8,128)(2,1)}, bf16[16,48,768]{2,1,0:T(8,128)(2,1)S(1)}, u32[]{:S(2)}, u32[]{:S(2)}) %collective-permute-start.11) | collective-permute-done | bytes 1179680 | tf_op jit(solution)/shard_map/ppermute | solution.py:1133
  59.4 1.0 copy-done.39
  60.4 31.6 %feed.1 = (f32[1568,384]{1,0:T(8,128)}, f32[8,208,384]{2,1,0:T(8,128)}, bf16[8,208,384]{2,1,0:T(8,128)(2,1)}, bf16[768,768]{1,0:T(8,128)(2,1)}, bf16[768,768]{1,...) custom-call(s32[2]{0:T(128)} %copy-done.14, s32[8,2]{1,0:T(8,128)} %copy.79.keep_ref, ...), custom_call_target="tpu_custom_call" | custom-call | flops 40249999360 | tf_op jit(solution)/shard_map/feed/pallas_call | solution.py:732
  92.5 2.7 %collective-permute-done.12.two_ref = bf16[768,768]{1,0:T(8,128)(2,1)S(1)} collective-permute-done((bf16[768,768]{1,0:T(8,128)(2,1)}, bf16[768,768]{1,0:T(8,128)(2,1)S(1)}, u32[]{:S(2)}, u32[]{:S(2)}) %collective-permute-start.12) | collective-permute-done | bytes 1179680 | tf_op jit(solution)/shard_map/ppermute | solution.py:1133
  95.1 1.3 copy-done.15
  96.4 1.1 add.251
  97.5 5.0 %all-to-all-start = ((bf16[16,48,768]{2,1,0:T(8,128)(2,1)}), bf16[16,48,768]{2,1,0:T(8,128)(2,1)S(1)}, u32[]{:S(2)}, u32[]{:S(2)}) async-start(bf16[16,48,768]{2,1,0:T(8,128)(2,1)} %bitcast.14), calls=%async_computation | async-start | bytes 2359296 | tf_op jit(solution)/shard_map/all_to_all | solution.py:1137
  102.5 30.9 %attend_backward.1 = (f32[1568,384]{1,0:T(8,128)}, bf16[17,24,768]{2,1,0:T(8,128)(2,1)}, bf16[17,24,768]{2,1,0:T(8,128)(2,1)}) custom-call(s32[2]{0:T(128)} %copy-done.14, bf16[8,208,384]{2,1,0:T(8,128)(2,1)} %copy-done.16, f32[8,208,384]{2,1,0:T(8,128)} %get-tuple-element.94.grad_ref, bf16[8,208,384]{2,1,0:T(8,128)(2,1)} %get-tuple-element.98.dout_ref, ...), custom_call_target="tpu_custom_call" | custom-call | flops 51749998592 | tf_op jit(solution)/shard_map/attend_backward/pallas_call | solution.py:1040
  133.4 0.7 collective-permute-start.13
  134.3 0.7 fusion.15
  135.1 0.7 fusion.17
  136.3 1.7 %collective-permute-start.14 = (bf16[112,768]{1,0:T(8,128)(2,1)S(1)}, bf16[112,768]{1,0:T(8,128)(2,1)S(1)}, u32[]{:S(2)}, u32[]{:S(2)}) collective-permute-start(bf16[112,768]{1,0:T(8,128)(2,1)S(1)} %get-tuple-element.159), channel_id=1, source_target_pairs={{0,2},{2,0},{4,6},{6,4},{8,10},{10,8},{12,14},{14,12},{16,18},{18,... | collective-permute-start | bytes 516104 | tf_op jit(solution)/shard_map/ppermute | solution.py:1123
  138.0 1.2 collective-permute-start.16
  140.0 2.4 %collective-permute-done.14 = bf16[112,768]{1,0:T(8,128)(2,1)S(1)} collective-permute-done((bf16[112,768]{1,0:T(8,128)(2,1)S(1)}, bf16[112,768]{1,0:T(8,128)(2,1)S(1)}, u32[]{:S(2)}, u32[]{:S(2)}) %collective-permute-start.14) | collective-permute-done | bytes 172064 | tf_op jit(solution)/shard_map/ppermute | solution.py:1123
  142.4 4.7 %collective-permute-done.16 = bf16[112,768]{1,0:T(8,128)(2,1)S(1)} collective-permute-done((bf16[112,768]{1,0:T(8,128)(2,1)S(1)}, bf16[112,768]{1,0:T(8,128)(2,1)S(1)}, u32[]{:S(2)}, u32[]{:S(2)}) %collective-permute-start.16) | collective-permute-done | bytes 172064 | tf_op jit(solution)/shard_map/ppermute | solution.py:1123
  147.3 1.2 collective-permute-start.17
  148.5 2.1 %collective-permute-start.18 = (bf16[40,768]{1,0:T(8,128)(2,1)S(1)}, bf16[40,768]{1,0:T(8,128)(2,1)S(1)}, u32[]{:S(2)}, u32[]{:S(2)}) collective-permute-start(bf16[40,768]{1,0:T(8,128)(2,1)S(1)} %get-tuple-element.157), channel_id=1, source_target_pairs={{0,16},{2,18},{4,20},{6,22},{8,24},{10,26},{12,28},{14,30},{16,0},... | collective-permute-start | bytes 184328 | tf_op jit(solution)/shard_map/ppermute | solution.py:1123
  150.9 0.6 multiply_add_fusion.2
  151.7 1.6 collective-permute-done.18
  153.3 3.0 %collective-permute-done.19 = bf16[40,768]{1,0:T(8,128)(2,1)S(1)} collective-permute-done((bf16[40,768]{1,0:T(8,128)(2,1)S(1)}, bf16[40,768]{1,0:T(8,128)(2,1)S(1)}, u32[]{:S(2)}, u32[]{:S(2)}) %collective-permute-start.19) | collective-permute-done | bytes 61472 | tf_op jit(solution)/shard_map/ppermute | solution.py:1123
  156.6 3.5 %collective-permute-start.20 = (f32[3,768]{1,0:T(4,128)S(1)}, f32[3,768]{1,0:T(4,128)S(1)}, u32[]{:S(2)}, u32[]{:S(2)}) collective-permute-start(f32[3,768]{1,0:T(4,128)S(1)} %slice.260), channel_id=1, source_target_pairs={{0,1},{1,0},{2,3},{3,2},{4,5},{5,4},{6,7},{7,6},{8,9},{9,8},{10,11... | collective-permute-start | bytes 27656 | tf_op jit(solution)/shard_map/ppermute | solution.py:1133
  161.2 0.7 multiply_add_fusion.6
  162.0 0.8 update.1
  163.2 0.7 multiply_add_fusion.4
  (174 shorter events, 6.8 us)
Async XLA Ops:
  0.7 26.6 %copy-start = (s32[16,2]{0,1:T(2,128)S(1)}, s32[16,2]{0,1:T(2,128)}, u32[]{:S(2)}) copy-start(s32[16,2]{0,1:T(2,128)} %param.38) | copy-start | bytes 388
  0.7 6.3 %copy-start.23 = (f32[6,530]{1,0:T(8,128)S(1)}, f32[6,530]{1,0:T(8,128)}, u32[]{:S(2)}) copy-start(f32[6,530]{1,0:T(8,128)} %param.44) | copy-start | bytes 38164
  0.7 7.6 %copy-start.1 = (bf16[3136,384]{1,0:T(8,128)(2,1)S(1)}, bf16[3136,384]{1,0:T(8,128)(2,1)}, u32[]{:S(2)}) copy-start(bf16[3136,384]{1,0:T(8,128)(2,1)} %tokens_ref.1) | copy-start | bytes 7225348
  2.6 11.9 %collective-permute-start.3 = (bf16[72,768]{1,0:T(8,128)(2,1)}, bf16[72,768]{1,0:T(8,128)(2,1)S(1)}, u32[]{:S(2)}, u32[]{:S(2)}) collective-permute-start(bf16[72,768]{1,0:T(8,128)(2,1)} %shard.1), channel_id=1, source_target_pairs={{0,24},{2,26},{4,28},{6,30},{8,16},{10,18},{12,20},{14,22},{16,8},... | collective-permute-start | bytes 331784 | tf_op jit(solution)/shard_map/ppermute | solution.py:1123
  6.7 9.1 %collective-permute-start.2 = (bf16[72,768]{1,0:T(8,128)(2,1)}, bf16[72,768]{1,0:T(8,128)(2,1)S(1)}, u32[]{:S(2)}, u32[]{:S(2)}) collective-permute-start(bf16[72,768]{1,0:T(8,128)(2,1)} %shard.1), channel_id=1, source_target_pairs={{0,16},{2,18},{4,20},{6,22},{8,24},{10,26},{12,28},{14,30},{16,0},... | collective-permute-start | bytes 331784 | tf_op jit(solution)/shard_map/ppermute | solution.py:1123
  6.7 9.1 %collective-permute-start.1 = (bf16[72,768]{1,0:T(8,128)(2,1)}, bf16[72,768]{1,0:T(8,128)(2,1)S(1)}, u32[]{:S(2)}, u32[]{:S(2)}) collective-permute-start(bf16[72,768]{1,0:T(8,128)(2,1)} %shard.1), channel_id=1, source_target_pairs={{0,8},{2,10},{4,12},{6,14},{8,0},{10,2},{12,4},{14,6},{16,24},{18,... | collective-permute-start | bytes 331784 | tf_op jit(solution)/shard_map/ppermute | solution.py:1123
  7.0 5.7 %collective-permute-start = (f32[6,530]{1,0:T(8,128)S(1)}, f32[6,530]{1,0:T(8,128)S(1)}, u32[]{:S(2)}, u32[]{:S(2)}) collective-permute-start(f32[6,530]{1,0:T(8,128)S(1)} %copy-done.23), channel_id=1, source_target_pairs={{0,1},{1,0},{2,3},{3,2},{4,5},{5,4},{6,7},{7,6},{8,9},{9,8},{10,11... | collective-permute-start | bytes 38168 | tf_op jit(solution)/shard_map/ppermute | solution.py:1133
  13.2 2.6 %copy-start.22 = (bf16[72,768]{1,0:T(8,128)(2,1)S(1)}, bf16[72,768]{1,0:T(8,128)(2,1)}, u32[]{:S(2)}) copy-start(bf16[72,768]{1,0:T(8,128)(2,1)} %shard.1) | copy-start | bytes 331780
  14.0 4.7 %copy-start.11 = (s32[192,256]{1,0:T(8,128)S(1)}, s32[192,256]{1,0:T(8,128)}, u32[]{:S(2)}) copy-start(s32[192,256]{1,0:T(8,128)} %constant.38.clone.kind_ref) | copy-start | bytes 589828
  14.0 4.7 %copy-start.12 = (f32[128,256]{1,0:T(8,128)S(1)}, f32[128,256]{1,0:T(8,128)}, u32[]{:S(2)}) copy-start(f32[128,256]{1,0:T(8,128)} %constant.40.clone.spread_ref) | copy-start | bytes 393220
  14.0 4.7 %copy-start.13 = (s32[56,128]{1,0:T(8,128)S(1)}, s32[56,128]{1,0:T(8,128)}, u32[]{:S(2)}) copy-start(s32[56,128]{1,0:T(8,128)} %constant.39.clone.far_kind_ref) | copy-start | bytes 86020
  15.9 7.0 %collective-permute-start.5 = (bf16[4,24,768]{2,1,0:T(8,128)(2,1)S(1)}, bf16[4,24,768]{2,1,0:T(8,128)(2,1)S(1)}, u32[]{:S(2)}, u32[]{:S(2)}) collective-permute-start(bf16[4,24,768]{2,1,0:T(8,128)(2,1)S(1)} %get-tuple-element.146), channel_id=1, source_target_pairs={{0,4},{2,6},{4,0},{6,2},{8,12},{10,14},{12,8},{14,10},{16,20},{18,... | collective-permute-start | bytes 442376 | tf_op jit(solution)/shard_map/ppermute | solution.py:1123
  17.2 5.7 %collective-permute-start.4 = (bf16[4,24,768]{2,1,0:T(8,128)(2,1)S(1)}, bf16[4,24,768]{2,1,0:T(8,128)(2,1)S(1)}, u32[]{:S(2)}, u32[]{:S(2)}) collective-permute-start(bf16[4,24,768]{2,1,0:T(8,128)(2,1)S(1)} %get-tuple-element.146), channel_id=1, source_target_pairs={{0,2},{2,0},{4,6},{6,4},{8,10},{10,8},{12,14},{14,12},{16,18},{18,... | collective-permute-start | bytes 442376 | tf_op jit(solution)/shard_map/ppermute | solution.py:1123
  18.4 6.8 %collective-permute-start.6 = (bf16[4,24,768]{2,1,0:T(8,128)(2,1)S(1)}, bf16[4,24,768]{2,1,0:T(8,128)(2,1)S(1)}, u32[]{:S(2)}, u32[]{:S(2)}) collective-permute-start(bf16[4,24,768]{2,1,0:T(8,128)(2,1)S(1)} %get-tuple-element.146), channel_id=1, source_target_pairs={{0,6},{2,4},{4,2},{6,0},{8,14},{10,12},{12,10},{14,8},{16,22},{18,... | collective-permute-start | bytes 442376 | tf_op jit(solution)/shard_map/ppermute | solution.py:1123
  25.3 5.4 %copy-start.19 = (bf16[4,4,24,768]{3,2,1,0:T(8,128)(2,1)}, bf16[4,4,24,768]{3,2,1,0:T(8,128)(2,1)S(1)}, u32[]{:S(2)}) copy-start(bf16[4,4,24,768]{3,2,1,0:T(8,128)(2,1)S(1)} %pad_maximum_fusion) | copy-start | bytes 1769476
  25.3 5.4 %collective-permute-start.10 = (bf16[16,24,768]{2,1,0:T(8,128)(2,1)S(1)}, bf16[16,24,768]{2,1,0:T(8,128)(2,1)S(1)}, u32[]{:S(2)}, u32[]{:S(2)}) collective-permute-start(bf16[16,24,768]{2,1,0:T(8,128)(2,1)S(1)} %bitcast.61), channel_id=1, source_target_pairs={{0,1},{1,0},{2,3},{3,2},{4,5},{5,4},{6,7},{7,6},{8,9},{9,8},{10,11... | collective-permute-start | bytes 1769480 | tf_op jit(solution)/shard_map/ppermute | solution.py:1133
  28.0 24.8 %collective-permute-start.9 = (bf16[4,48,768]{2,1,0:T(8,128)(2,1)S(1)}, bf16[4,48,768]{2,1,0:T(8,128)(2,1)S(1)}, u32[]{:S(2)}, u32[]{:S(2)}) collective-permute-start(bf16[4,48,768]{2,1,0:T(8,128)(2,1)S(1)} %slice.182), channel_id=1, source_target_pairs={{0,6},{2,4},{4,2},{6,0},{8,14},{10,12},{12,10},{14,8},{16,22},{18,... | collective-permute-start | bytes 884744 | tf_op jit(solution)/shard_map/ppermute | solution.py:1123
  29.7 23.2 %collective-permute-start.8 = (bf16[4,48,768]{2,1,0:T(8,128)(2,1)S(1)}, bf16[4,48,768]{2,1,0:T(8,128)(2,1)S(1)}, u32[]{:S(2)}, u32[]{:S(2)}) collective-permute-start(bf16[4,48,768]{2,1,0:T(8,128)(2,1)S(1)} %slice.182), channel_id=1, source_target_pairs={{0,4},{2,6},{4,0},{6,2},{8,12},{10,14},{12,8},{14,10},{16,20},{18,... | collective-permute-start | bytes 884744 | tf_op jit(solution)/shard_map/ppermute | solution.py:1123
  29.9 23.0 %collective-permute-start.7 = (bf16[4,48,768]{2,1,0:T(8,128)(2,1)S(1)}, bf16[4,48,768]{2,1,0:T(8,128)(2,1)S(1)}, u32[]{:S(2)}, u32[]{:S(2)}) collective-permute-start(bf16[4,48,768]{2,1,0:T(8,128)(2,1)S(1)} %slice.182), channel_id=1, source_target_pairs={{0,2},{2,0},{4,6},{6,4},{8,10},{10,8},{12,14},{14,12},{16,18},{18,... | collective-permute-start | bytes 884744 | tf_op jit(solution)/shard_map/ppermute | solution.py:1123
  52.8 3.8 %slice-start = ((f32[12,384]{1,0:T(8,128)}), f32[4,384]{1,0:T(4,128)S(1)}, s32[]{:S(2)}) async-start(f32[12,384]{1,0:T(8,128)} %vec_ref.5), calls=%async_computation.1 | async-start | bytes 12288 | tf_op jit(solution)/shard_map/slice | solution.py:1239
  55.8 3.6 %collective-permute-start.11 = (bf16[16,48,768]{2,1,0:T(8,128)(2,1)}, bf16[16,48,768]{2,1,0:T(8,128)(2,1)S(1)}, u32[]{:S(2)}, u32[]{:S(2)}) collective-permute-start(bf16[16,48,768]{2,1,0:T(8,128)(2,1)} %constant_dynamic-update-slice_fusion.ff0_ref), channel_id=1, source_target_pairs={{0,1},{1,0},{2,3},{3,2},{4,5},{5,4},{6,7},{7,6},{8,9},{9,8},{10,11... | collective-permute-start | bytes 3538952 | tf_op jit(solution)/shard_map/ppermute | solution.py:1133
  92.0 3.1 %collective-permute-start.12 = (bf16[768,768]{1,0:T(8,128)(2,1)}, bf16[768,768]{1,0:T(8,128)(2,1)S(1)}, u32[]{:S(2)}, u32[]{:S(2)}) collective-permute-start(bf16[768,768]{1,0:T(8,128)(2,1)} %get-tuple-element.96), channel_id=1, source_target_pairs={{0,1},{1,0},{2,3},{3,2},{4,5},{5,4},{6,7},{7,6},{8,9},{9,8},{10,11... | collective-permute-start | bytes 3538952 | tf_op jit(solution)/shard_map/ppermute | solution.py:1133
  97.5 35.9 %all-to-all-start = ((bf16[16,48,768]{2,1,0:T(8,128)(2,1)}), bf16[16,48,768]{2,1,0:T(8,128)(2,1)S(1)}, u32[]{:S(2)}, u32[]{:S(2)}) async-start(bf16[16,48,768]{2,1,0:T(8,128)(2,1)} %bitcast.14), calls=%async_computation | async-start | bytes 2359296 | tf_op jit(solution)/shard_map/all_to_all | solution.py:1137
  133.4 1.7 %copy-start.27 = (f32[384,48]{0,1:T(8,128)S(1)}, f32[384,48]{0,1:T(8,128)}, u32[]{:S(2)}) copy-start(f32[384,48]{0,1:T(8,128)} %param.42) | copy-start | bytes 221188
  133.4 2.6 %copy-start.18 = (bf16[17,24,768]{2,1,0:T(8,128)(2,1)S(1)}, bf16[17,24,768]{2,1,0:T(8,128)(2,1)}, u32[]{:S(2)}) copy-start(bf16[17,24,768]{2,1,0:T(8,128)(2,1)} %get-tuple-element.107) | copy-start | bytes 1880068
  133.4 2.6 %collective-permute-start.13 = (bf16[17,24,768]{2,1,0:T(8,128)(2,1)}, bf16[17,24,768]{2,1,0:T(8,128)(2,1)S(1)}, u32[]{:S(2)}, u32[]{:S(2)}) collective-permute-start(bf16[17,24,768]{2,1,0:T(8,128)(2,1)} %get-tuple-element.110), channel_id=1, source_target_pairs={{0,1},{1,0},{2,3},{3,2},{4,5},{5,4},{6,7},{7,6},{8,9},{9,8},{10,11... | collective-permute-start | bytes 1880072 | tf_op jit(solution)/shard_map/ppermute | solution.py:1133
  135.1 4.2 %copy-start.20 = (f32[48,384]{1,0:T(8,128)}, f32[48,384]{1,0:T(8,128)S(1)}, u32[]{:S(2)}) copy-start(f32[48,384]{1,0:T(8,128)S(1)} %get-tuple-element.131) | copy-start | bytes 221188
  135.8 15.1 %copy-start.21 = (f32[384,48]{0,1:T(8,128)}, f32[384,48]{0,1:T(8,128)S(1)}, u32[]{:S(2)}) copy-start(f32[384,48]{0,1:T(8,128)S(1)} %get-tuple-element.135) | copy-start | bytes 221188
  136.2 3.1 %copy-start.30 = (f32[48,384]{1,0:T(8,128)S(1)}, f32[48,384]{1,0:T(8,128)}, u32[]{:S(2)}) copy-start(f32[48,384]{1,0:T(8,128)} %param.57) | copy-start | bytes 221188
  136.3 6.0 %collective-permute-start.14 = (bf16[112,768]{1,0:T(8,128)(2,1)S(1)}, bf16[112,768]{1,0:T(8,128)(2,1)S(1)}, u32[]{:S(2)}, u32[]{:S(2)}) collective-permute-start(bf16[112,768]{1,0:T(8,128)(2,1)S(1)} %get-tuple-element.159), channel_id=1, source_target_pairs={{0,2},{2,0},{4,6},{6,4},{8,10},{10,8},{12,14},{14,12},{16,18},{18,... | collective-permute-start | bytes 516104 | tf_op jit(solution)/shard_map/ppermute | solution.py:1123
  138.0 9.0 %collective-permute-start.16 = (bf16[112,768]{1,0:T(8,128)(2,1)S(1)}, bf16[112,768]{1,0:T(8,128)(2,1)S(1)}, u32[]{:S(2)}, u32[]{:S(2)}) collective-permute-start(bf16[112,768]{1,0:T(8,128)(2,1)S(1)} %get-tuple-element.160), channel_id=1, source_target_pairs={{0,6},{2,4},{4,2},{6,0},{8,14},{10,12},{12,10},{14,8},{16,22},{18,... | collective-permute-start | bytes 516104 | tf_op jit(solution)/shard_map/ppermute | solution.py:1123
  139.2 7.9 %collective-permute-start.15 = (bf16[112,768]{1,0:T(8,128)(2,1)S(1)}, bf16[112,768]{1,0:T(8,128)(2,1)S(1)}, u32[]{:S(2)}, u32[]{:S(2)}) collective-permute-start(bf16[112,768]{1,0:T(8,128)(2,1)S(1)} %get-tuple-element.161), channel_id=1, source_target_pairs={{0,4},{2,6},{4,0},{6,2},{8,12},{10,14},{12,8},{14,10},{16,20},{18,... | collective-permute-start | bytes 516104 | tf_op jit(solution)/shard_map/ppermute | solution.py:1123
  147.1 3.8 %copy-start.31 = (f32[384,48]{0,1:T(8,128)S(1)}, f32[384,48]{0,1:T(8,128)}, u32[]{:S(2)}) copy-start(f32[384,48]{0,1:T(8,128)} %param.54) | copy-start | bytes 221188
  147.3 4.3 %collective-permute-start.17 = (bf16[40,768]{1,0:T(8,128)(2,1)S(1)}, bf16[40,768]{1,0:T(8,128)(2,1)S(1)}, u32[]{:S(2)}, u32[]{:S(2)}) collective-permute-start(bf16[40,768]{1,0:T(8,128)(2,1)S(1)} %get-tuple-element.156), channel_id=1, source_target_pairs={{0,8},{2,10},{4,12},{6,14},{8,0},{10,2},{12,4},{14,6},{16,24},{18,... | collective-permute-start | bytes 184328 | tf_op jit(solution)/shard_map/ppermute | solution.py:1123
  148.5 4.7 %collective-permute-start.18 = (bf16[40,768]{1,0:T(8,128)(2,1)S(1)}, bf16[40,768]{1,0:T(8,128)(2,1)S(1)}, u32[]{:S(2)}, u32[]{:S(2)}) collective-permute-start(bf16[40,768]{1,0:T(8,128)(2,1)S(1)} %get-tuple-element.157), channel_id=1, source_target_pairs={{0,16},{2,18},{4,20},{6,22},{8,24},{10,26},{12,28},{14,30},{16,0},... | collective-permute-start | bytes 184328 | tf_op jit(solution)/shard_map/ppermute | solution.py:1123
  150.6 5.6 %collective-permute-start.19 = (bf16[40,768]{1,0:T(8,128)(2,1)S(1)}, bf16[40,768]{1,0:T(8,128)(2,1)S(1)}, u32[]{:S(2)}, u32[]{:S(2)}) collective-permute-start(bf16[40,768]{1,0:T(8,128)(2,1)S(1)} %get-tuple-element.158), channel_id=1, source_target_pairs={{0,24},{2,26},{4,28},{6,30},{8,16},{10,18},{12,20},{14,22},{16,8},... | collective-permute-start | bytes 184328 | tf_op jit(solution)/shard_map/ppermute | solution.py:1123
  151.6 9.6 %copy-start.36 = (f32[6,530]{1,0:T(8,128)S(1)}, f32[6,530]{1,0:T(8,128)}, u32[]{:S(2)}) copy-start(f32[6,530]{1,0:T(8,128)} %param.60) | copy-start | bytes 38164
  151.6 9.6 %copy-start.37 = (f32[6,530]{1,0:T(8,128)S(1)}, f32[6,530]{1,0:T(8,128)}, u32[]{:S(2)}) copy-start(f32[6,530]{1,0:T(8,128)} %param.58) | copy-start | bytes 38164
  151.6 9.6 %copy-start.38 = (f32[6,530]{1,0:T(8,128)S(1)}, f32[6,530]{1,0:T(8,128)}, u32[]{:S(2)}) copy-start(f32[6,530]{1,0:T(8,128)} %param.59) | copy-start | bytes 38164
  151.6 10.3 %copy-start.3 = (f32[3,24,192]{2,1,0:T(8,128)S(1)}, f32[3,24,192]{2,1,0:T(8,128)}, u32[]{:S(2)}) copy-start(f32[3,24,192]{2,1,0:T(8,128)} %refs_0_.1) | copy-start | bytes 165892
  151.6 10.3 %copy-start.4 = (f32[3,24,192]{2,1,0:T(8,128)S(1)}, f32[3,24,192]{2,1,0:T(8,128)}, u32[]{:S(2)}) copy-start(f32[3,24,192]{2,1,0:T(8,128)} %refs_1_.1) | copy-start | bytes 165892
  151.6 10.3 %copy-start.5 = (f32[3,24,192]{2,1,0:T(8,128)S(1)}, f32[3,24,192]{2,1,0:T(8,128)}, u32[]{:S(2)}) copy-start(f32[3,24,192]{2,1,0:T(8,128)} %refs_2_.1) | copy-start | bytes 165892
  151.6 10.3 %copy-start.6 = (f32[3,24,192]{2,1,0:T(8,128)S(1)}, f32[3,24,192]{2,1,0:T(8,128)}, u32[]{:S(2)}) copy-start(f32[3,24,192]{2,1,0:T(8,128)} %refs_3_.1) | copy-start | bytes 165892
  151.6 10.3 %copy-start.7 = (f32[192,24]{0,1:T(8,128)S(1)}, f32[192,24]{0,1:T(8,128)}, u32[]{:S(2)}) copy-start(f32[192,24]{0,1:T(8,128)} %param.41) | copy-start | bytes 55300
  151.7 10.3 %copy-start.8 = (f32[192,24]{0,1:T(8,128)S(1)}, f32[192,24]{0,1:T(8,128)}, u32[]{:S(2)}) copy-start(f32[192,24]{0,1:T(8,128)} %param.49) | copy-start | bytes 55300
  151.7 10.3 %copy-start.9 = (f32[192,24]{0,1:T(8,128)S(1)}, f32[192,24]{0,1:T(8,128)}, u32[]{:S(2)}) copy-start(f32[192,24]{0,1:T(8,128)} %param.50) | copy-start | bytes 55300
  151.7 10.3 %copy-start.10 = (f32[192,24]{0,1:T(8,128)S(1)}, f32[192,24]{0,1:T(8,128)}, u32[]{:S(2)}) copy-start(f32[192,24]{0,1:T(8,128)} %param.51) | copy-start | bytes 55300
  156.6 6.2 %collective-permute-start.20 = (f32[3,768]{1,0:T(4,128)S(1)}, f32[3,768]{1,0:T(4,128)S(1)}, u32[]{:S(2)}, u32[]{:S(2)}) collective-permute-start(f32[3,768]{1,0:T(4,128)S(1)} %slice.260), channel_id=1, source_target_pairs={{0,1},{1,0},{2,3},{3,2},{4,5},{5,4},{6,7},{7,6},{8,9},{9,8},{10,11... | collective-permute-start | bytes 27656 | tf_op jit(solution)/shard_map/ppermute | solution.py:1133
  (16 other events, 18.4 us)

commit v2 on v1

--- a/solution.py
+++ b/solution.py
@@ -1088,7 +1088,7 @@
             ],
         ),
         out_shape=[jax.ShapeDtypeStruct(s, d) for s, d in shapes],
-        compiler_params=params(60),
+        compiler_params=params(56),
         cost_estimate=cost(45),
         name="attend_backward",
     )(

time: 164 us -> 164 us (level)
  no operation moved by 1% of the time
where the time goes in v2:
time: 164 us
  Pallas kernels  92.7 us (57%)
  starting transfers between devices  30.1 us (18%)
  waiting for transfers between devices  20.1 us (12%)
  local copies, waits for them, and re-layouts  14.1 us (9%)
  other arithmetic  5.24 us (3%)
    pallas_call x1, Pallas kernels, feed(): pl.pallas_call(feed_kernel, grid_spec=pltpu.PrefetchScalarGridSpec(num_sc...  31.6 us
    pallas_call x1, Pallas kernels, attend_backward(): pl.pallas_call(backward_kernel, grid_spec=pltpu.PrefetchScalarGridSpec(nu...  30.9 us
    pallas_call x1, Pallas kernels, attend_forward(): pl.pallas_call(forward_kernel, grid_spec=pltpu.PrefetchScalarGridSpec(num...  21.3 us
    ppermute x15, starting transfers between devices, hop(): lax.ppermute(v, 'dp', [(i, i ^ mask * stride) for i in range(lax.axis_siz...  16.4 us
    ppermute x15, waiting for transfers between devices, hop(): lax.ppermute(v, 'dp', [(i, i ^ mask * stride) for i in range(lax.axis_siz...  15.3 us
    unnamed x88, local copies, waits for them, and re-layouts  9.86 us
    ppermute x6, starting transfers between devices, swap(): return lax.ppermute(v, 'head', [(0, 1), (1, 0)])  8.76 us
    all_to_all x1, starting transfers between devices, exchange(): return lax.all_to_all(v, 'dp', 0, 0)  4.98 us
  transfers between devices with their start and end apart: 22, of which 9 were waited for; matrix products, arithmetic and copies ran while one was open for 5% of the time, Pallas kernels for 35%

profile of v2, /device:TPU:1, one launch (start us, length us, event | category | flops | bytes accessed | tf_op | source)
XLA Modules:
  0.0 163.8 jit_solution(16454186280802932847)
XLA Ops:
  0.7 1.8 %shard.1 = bf16[72,768]{1,0:T(8,128)(2,1)} custom-call(f32[3,24,192]{2,1,0:T(8,128)} %refs_0_.1, f32[24,192]{1,0:T(8,128)} %bitcast.54, f32[48,384]{1,0:T(8,128)} %bitcast.74, f32[48,384]{1,0:T(8,128)} %shrink_ref.1), custom_call_target="tpu_custom_call" | custom-call | flops 1150000000 | tf_op jit(solution)/shard_map/shard/pallas_call | solution.py:318
  2.6 4.2 %collective-permute-start.3 = (bf16[72,768]{1,0:T(8,128)(2,1)}, bf16[72,768]{1,0:T(8,128)(2,1)S(1)}, u32[]{:S(2)}, u32[]{:S(2)}) collective-permute-start(bf16[72,768]{1,0:T(8,128)(2,1)} %shard.1), channel_id=1, source_target_pairs={{0,24},{2,26},{4,28},{6,30},{8,16},{10,18},{12,20},{14,22},{16,8},... | collective-permute-start | bytes 331784 | tf_op jit(solution)/shard_map/ppermute | solution.py:1123
  7.0 1.2 collective-permute-start
  8.3 1.3 copy-done.2
  9.6 0.9 prepare.1
  10.5 1.1 copy-done.16
  11.6 1.2 copy-done.17
  14.5 1.3 collective-permute-done.2
  15.9 1.3 collective-permute-start.5
  17.2 1.2 collective-permute-start.4
  18.7 4.2 %spread_tables.1.bias_ref = f32[12,192,256]{2,1,0:T(8,128)} custom-call(f32[3,4,1024]{2,1,0:T(4,128)S(1)} %reshape.141.line_ref, s32[192,256]{1,0:T(8,128)S(1)} %copy-done.11, s32[56,128]{1,0:T(8,128)S(1)} %copy-done.13, f32[128,256]{1,0:T(8,128)S(1)} %copy-done.12), custom_call_target="tpu_custom_call" | custom-call | flops 8049999872 | tf_op jit(solution)/shard_map/spread_tables/pallas_call | solution.py:183
  22.9 2.3 %collective-permute-done.6 = bf16[4,24,768]{2,1,0:T(8,128)(2,1)S(1)} collective-permute-done((bf16[4,24,768]{2,1,0:T(8,128)(2,1)S(1)}, bf16[4,24,768]{2,1,0:T(8,128)(2,1)S(1)}, u32[]{:S(2)}, u32[]{:S(2)}) %collective-permute-start.6) | collective-permute-done | bytes 147488 | tf_op jit(solution)/shard_map/ppermute | solution.py:1123
  25.3 2.0 %collective-permute-start.10 = (bf16[16,24,768]{2,1,0:T(8,128)(2,1)S(1)}, bf16[16,24,768]{2,1,0:T(8,128)(2,1)S(1)}, u32[]{:S(2)}, u32[]{:S(2)}) collective-permute-start(bf16[16,24,768]{2,1,0:T(8,128)(2,1)S(1)} %bitcast.61), channel_id=1, source_target_pairs={{0,1},{1,0},{2,3},{3,2},{4,5},{5,4},{6,7},{7,6},{8,9},{9,8},{10,11... | collective-permute-start | bytes 1769480 | tf_op jit(solution)/shard_map/ppermute | solution.py:1133
  27.4 0.7 copy.79.keep_ref
  28.0 1.6 %collective-permute-start.9 = (bf16[4,48,768]{2,1,0:T(8,128)(2,1)S(1)}, bf16[4,48,768]{2,1,0:T(8,128)(2,1)S(1)}, u32[]{:S(2)}, u32[]{:S(2)}) collective-permute-start(bf16[4,48,768]{2,1,0:T(8,128)(2,1)S(1)} %slice.182), channel_id=1, source_target_pairs={{0,6},{2,4},{4,2},{6,0},{8,14},{10,12},{12,10},{14,8},{16,22},{18,... | collective-permute-start | bytes 884744 | tf_op jit(solution)/shard_map/ppermute | solution.py:1123
  29.9 0.8 collective-permute-start.7
  30.7 0.8 copy-done.40
  31.5 21.3 %attend_forward.1 = (f32[8,208,384]{2,1,0:T(8,128)}, bf16[8,208,384]{2,1,0:T(8,128)(2,1)}, bf16[8,12,192,256]{3,2,1,0:T(8,128)(2,1)}, bf16[8,208,384]{2,1,0:T(8,...) custom-call(s32[2]{0:T(128)} %copy-done.14, ...), custom_call_target="tpu_custom_call" | custom-call | flops 28750000128 | tf_op jit(solution)/shard_map/attend_forward/pallas_call | solution.py:560
  52.9 0.7 constant_dynamic-update-slice_fusion.3
  53.6 0.7 constant_dynamic-update-slice_fusion.2
  54.3 0.7 constant_dynamic-update-slice_fusion.1
  55.1 0.7 constant_dynamic-update-slice_fusion.ff0_ref
  55.8 0.9 collective-permute-start.11
  56.8 0.7 reshape.144.fb_ref
  57.5 1.9 %collective-permute-done.11.ff1_ref = bf16[16,48,768]{2,1,0:T(8,128)(2,1)S(1)} collective-permute-done((bf16[16,48,768]{2,1,0:T(8,128)(2,1)}, bf16[16,48,768]{2,1,0:T(8,128)(2,1)S(1)}, u32[]{:S(2)}, u32[]{:S(2)}) %collective-permute-start.11) | collective-permute-done | bytes 1179680 | tf_op jit(solution)/shard_map/ppermute | solution.py:1133
  59.4 1.0 copy-done.39
  60.4 31.6 %feed.1 = (f32[1568,384]{1,0:T(8,128)}, f32[8,208,384]{2,1,0:T(8,128)}, bf16[8,208,384]{2,1,0:T(8,128)(2,1)}, bf16[768,768]{1,0:T(8,128)(2,1)}, bf16[768,768]{1,...) custom-call(s32[2]{0:T(128)} %copy-done.14, s32[8,2]{1,0:T(8,128)} %copy.79.keep_ref, ...), custom_call_target="tpu_custom_call" | custom-call | flops 40249999360 | tf_op jit(solution)/shard_map/feed/pallas_call | solution.py:732
  92.5 2.7 %collective-permute-done.12.two_ref = bf16[768,768]{1,0:T(8,128)(2,1)S(1)} collective-permute-done((bf16[768,768]{1,0:T(8,128)(2,1)}, bf16[768,768]{1,0:T(8,128)(2,1)S(1)}, u32[]{:S(2)}, u32[]{:S(2)}) %collective-permute-start.12) | collective-permute-done | bytes 1179680 | tf_op jit(solution)/shard_map/ppermute | solution.py:1133
  95.1 1.3 copy-done.15
  96.4 1.1 add.251
  97.5 5.0 %all-to-all-start = ((bf16[16,48,768]{2,1,0:T(8,128)(2,1)}), bf16[16,48,768]{2,1,0:T(8,128)(2,1)S(1)}, u32[]{:S(2)}, u32[]{:S(2)}) async-start(bf16[16,48,768]{2,1,0:T(8,128)(2,1)} %bitcast.14), calls=%async_computation | async-start | bytes 2359296 | tf_op jit(solution)/shard_map/all_to_all | solution.py:1137
  102.5 30.9 %attend_backward.1 = (f32[1568,384]{1,0:T(8,128)}, bf16[17,24,768]{2,1,0:T(8,128)(2,1)}, bf16[17,24,768]{2,1,0:T(8,128)(2,1)}) custom-call(s32[2]{0:T(128)} %copy-done.14, bf16[8,208,384]{2,1,0:T(8,128)(2,1)} %copy-done.16, f32[8,208,384]{2,1,0:T(8,128)} %get-tuple-element.94.grad_ref, bf16[8,208,384]{2,1,0:T(8,128)(2,1)} %get-tuple-element.98.dout_ref, ...), custom_call_target="tpu_custom_call" | custom-call | flops 51749998592 | tf_op jit(solution)/shard_map/attend_backward/pallas_call | solution.py:1040
  133.4 0.7 collective-permute-start.13
  134.3 0.7 fusion.15
  135.1 0.7 fusion.17
  136.3 1.7 %collective-permute-start.14 = (bf16[112,768]{1,0:T(8,128)(2,1)S(1)}, bf16[112,768]{1,0:T(8,128)(2,1)S(1)}, u32[]{:S(2)}, u32[]{:S(2)}) collective-permute-start(bf16[112,768]{1,0:T(8,128)(2,1)S(1)} %get-tuple-element.159), channel_id=1, source_target_pairs={{0,2},{2,0},{4,6},{6,4},{8,10},{10,8},{12,14},{14,12},{16,18},{18,... | collective-permute-start | bytes 516104 | tf_op jit(solution)/shard_map/ppermute | solution.py:1123
  138.0 1.2 collective-permute-start.16
  140.0 2.4 %collective-permute-done.14 = bf16[112,768]{1,0:T(8,128)(2,1)S(1)} collective-permute-done((bf16[112,768]{1,0:T(8,128)(2,1)S(1)}, bf16[112,768]{1,0:T(8,128)(2,1)S(1)}, u32[]{:S(2)}, u32[]{:S(2)}) %collective-permute-start.14) | collective-permute-done | bytes 172064 | tf_op jit(solution)/shard_map/ppermute | solution.py:1123
  142.4 4.7 %collective-permute-done.16 = bf16[112,768]{1,0:T(8,128)(2,1)S(1)} collective-permute-done((bf16[112,768]{1,0:T(8,128)(2,1)S(1)}, bf16[112,768]{1,0:T(8,128)(2,1)S(1)}, u32[]{:S(2)}, u32[]{:S(2)}) %collective-permute-start.16) | collective-permute-done | bytes 172064 | tf_op jit(solution)/shard_map/ppermute | solution.py:1123
  147.3 1.2 collective-permute-start.17
  148.5 2.1 %collective-permute-start.18 = (bf16[40,768]{1,0:T(8,128)(2,1)S(1)}, bf16[40,768]{1,0:T(8,128)(2,1)S(1)}, u32[]{:S(2)}, u32[]{:S(2)}) collective-permute-start(bf16[40,768]{1,0:T(8,128)(2,1)S(1)} %get-tuple-element.157), channel_id=1, source_target_pairs={{0,16},{2,18},{4,20},{6,22},{8,24},{10,26},{12,28},{14,30},{16,0},... | collective-permute-start | bytes 184328 | tf_op jit(solution)/shard_map/ppermute | solution.py:1123
  150.9 0.6 multiply_add_fusion.2
  151.7 1.6 collective-permute-done.18
  153.3 3.0 %collective-permute-done.19 = bf16[40,768]{1,0:T(8,128)(2,1)S(1)} collective-permute-done((bf16[40,768]{1,0:T(8,128)(2,1)S(1)}, bf16[40,768]{1,0:T(8,128)(2,1)S(1)}, u32[]{:S(2)}, u32[]{:S(2)}) %collective-permute-start.19) | collective-permute-done | bytes 61472 | tf_op jit(solution)/shard_map/ppermute | solution.py:1123
  156.6 3.5 %collective-permute-start.20 = (f32[3,768]{1,0:T(4,128)S(1)}, f32[3,768]{1,0:T(4,128)S(1)}, u32[]{:S(2)}, u32[]{:S(2)}) collective-permute-start(f32[3,768]{1,0:T(4,128)S(1)} %slice.260), channel_id=1, source_target_pairs={{0,1},{1,0},{2,3},{3,2},{4,5},{5,4},{6,7},{7,6},{8,9},{9,8},{10,11... | collective-permute-start | bytes 27656 | tf_op jit(solution)/shard_map/ppermute | solution.py:1133
  161.2 0.7 multiply_add_fusion.6
  162.0 0.8 update.1
  163.2 0.7 multiply_add_fusion.4
  (174 shorter events, 6.8 us)
Async XLA Ops:
  0.7 26.6 %copy-start = (s32[16,2]{0,1:T(2,128)S(1)}, s32[16,2]{0,1:T(2,128)}, u32[]{:S(2)}) copy-start(s32[16,2]{0,1:T(2,128)} %param.38) | copy-start | bytes 388
  0.7 6.3 %copy-start.23 = (f32[6,530]{1,0:T(8,128)S(1)}, f32[6,530]{1,0:T(8,128)}, u32[]{:S(2)}) copy-start(f32[6,530]{1,0:T(8,128)} %param.44) | copy-start | bytes 38164
  0.7 7.6 %copy-start.1 = (bf16[3136,384]{1,0:T(8,128)(2,1)S(1)}, bf16[3136,384]{1,0:T(8,128)(2,1)}, u32[]{:S(2)}) copy-start(bf16[3136,384]{1,0:T(8,128)(2,1)} %tokens_ref.1) | copy-start | bytes 7225348
  2.6 11.9 %collective-permute-start.3 = (bf16[72,768]{1,0:T(8,128)(2,1)}, bf16[72,768]{1,0:T(8,128)(2,1)S(1)}, u32[]{:S(2)}, u32[]{:S(2)}) collective-permute-start(bf16[72,768]{1,0:T(8,128)(2,1)} %shard.1), channel_id=1, source_target_pairs={{0,24},{2,26},{4,28},{6,30},{8,16},{10,18},{12,20},{14,22},{16,8},... | collective-permute-start | bytes 331784 | tf_op jit(solution)/shard_map/ppermute | solution.py:1123
  6.7 9.1 %collective-permute-start.2 = (bf16[72,768]{1,0:T(8,128)(2,1)}, bf16[72,768]{1,0:T(8,128)(2,1)S(1)}, u32[]{:S(2)}, u32[]{:S(2)}) collective-permute-start(bf16[72,768]{1,0:T(8,128)(2,1)} %shard.1), channel_id=1, source_target_pairs={{0,16},{2,18},{4,20},{6,22},{8,24},{10,26},{12,28},{14,30},{16,0},... | collective-permute-start | bytes 331784 | tf_op jit(solution)/shard_map/ppermute | solution.py:1123
  6.7 9.1 %collective-permute-start.1 = (bf16[72,768]{1,0:T(8,128)(2,1)}, bf16[72,768]{1,0:T(8,128)(2,1)S(1)}, u32[]{:S(2)}, u32[]{:S(2)}) collective-permute-start(bf16[72,768]{1,0:T(8,128)(2,1)} %shard.1), channel_id=1, source_target_pairs={{0,8},{2,10},{4,12},{6,14},{8,0},{10,2},{12,4},{14,6},{16,24},{18,... | collective-permute-start | bytes 331784 | tf_op jit(solution)/shard_map/ppermute | solution.py:1123
  7.0 5.7 %collective-permute-start = (f32[6,530]{1,0:T(8,128)S(1)}, f32[6,530]{1,0:T(8,128)S(1)}, u32[]{:S(2)}, u32[]{:S(2)}) collective-permute-start(f32[6,530]{1,0:T(8,128)S(1)} %copy-done.23), channel_id=1, source_target_pairs={{0,1},{1,0},{2,3},{3,2},{4,5},{5,4},{6,7},{7,6},{8,9},{9,8},{10,11... | collective-permute-start | bytes 38168 | tf_op jit(solution)/shard_map/ppermute | solution.py:1133
  13.2 2.6 %copy-start.22 = (bf16[72,768]{1,0:T(8,128)(2,1)S(1)}, bf16[72,768]{1,0:T(8,128)(2,1)}, u32[]{:S(2)}) copy-start(bf16[72,768]{1,0:T(8,128)(2,1)} %shard.1) | copy-start | bytes 331780
  14.0 4.7 %copy-start.11 = (s32[192,256]{1,0:T(8,128)S(1)}, s32[192,256]{1,0:T(8,128)}, u32[]{:S(2)}) copy-start(s32[192,256]{1,0:T(8,128)} %constant.38.clone.kind_ref) | copy-start | bytes 589828
  14.0 4.7 %copy-start.12 = (f32[128,256]{1,0:T(8,128)S(1)}, f32[128,256]{1,0:T(8,128)}, u32[]{:S(2)}) copy-start(f32[128,256]{1,0:T(8,128)} %constant.40.clone.spread_ref) | copy-start | bytes 393220
  14.0 4.7 %copy-start.13 = (s32[56,128]{1,0:T(8,128)S(1)}, s32[56,128]{1,0:T(8,128)}, u32[]{:S(2)}) copy-start(s32[56,128]{1,0:T(8,128)} %constant.39.clone.far_kind_ref) | copy-start | bytes 86020
  15.9 7.0 %collective-permute-start.5 = (bf16[4,24,768]{2,1,0:T(8,128)(2,1)S(1)}, bf16[4,24,768]{2,1,0:T(8,128)(2,1)S(1)}, u32[]{:S(2)}, u32[]{:S(2)}) collective-permute-start(bf16[4,24,768]{2,1,0:T(8,128)(2,1)S(1)} %get-tuple-element.146), channel_id=1, source_target_pairs={{0,4},{2,6},{4,0},{6,2},{8,12},{10,14},{12,8},{14,10},{16,20},{18,... | collective-permute-start | bytes 442376 | tf_op jit(solution)/shard_map/ppermute | solution.py:1123
  17.2 5.7 %collective-permute-start.4 = (bf16[4,24,768]{2,1,0:T(8,128)(2,1)S(1)}, bf16[4,24,768]{2,1,0:T(8,128)(2,1)S(1)}, u32[]{:S(2)}, u32[]{:S(2)}) collective-permute-start(bf16[4,24,768]{2,1,0:T(8,128)(2,1)S(1)} %get-tuple-element.146), channel_id=1, source_target_pairs={{0,2},{2,0},{4,6},{6,4},{8,10},{10,8},{12,14},{14,12},{16,18},{18,... | collective-permute-start | bytes 442376 | tf_op jit(solution)/shard_map/ppermute | solution.py:1123
  18.4 6.8 %collective-permute-start.6 = (bf16[4,24,768]{2,1,0:T(8,128)(2,1)S(1)}, bf16[4,24,768]{2,1,0:T(8,128)(2,1)S(1)}, u32[]{:S(2)}, u32[]{:S(2)}) collective-permute-start(bf16[4,24,768]{2,1,0:T(8,128)(2,1)S(1)} %get-tuple-element.146), channel_id=1, source_target_pairs={{0,6},{2,4},{4,2},{6,0},{8,14},{10,12},{12,10},{14,8},{16,22},{18,... | collective-permute-start | bytes 442376 | tf_op jit(solution)/shard_map/ppermute | solution.py:1123
  25.3 5.4 %copy-start.19 = (bf16[4,4,24,768]{3,2,1,0:T(8,128)(2,1)}, bf16[4,4,24,768]{3,2,1,0:T(8,128)(2,1)S(1)}, u32[]{:S(2)}) copy-start(bf16[4,4,24,768]{3,2,1,0:T(8,128)(2,1)S(1)} %pad_maximum_fusion) | copy-start | bytes 1769476
  25.3 5.4 %collective-permute-start.10 = (bf16[16,24,768]{2,1,0:T(8,128)(2,1)S(1)}, bf16[16,24,768]{2,1,0:T(8,128)(2,1)S(1)}, u32[]{:S(2)}, u32[]{:S(2)}) collective-permute-start(bf16[16,24,768]{2,1,0:T(8,128)(2,1)S(1)} %bitcast.61), channel_id=1, source_target_pairs={{0,1},{1,0},{2,3},{3,2},{4,5},{5,4},{6,7},{7,6},{8,9},{9,8},{10,11... | collective-permute-start | bytes 1769480 | tf_op jit(solution)/shard_map/ppermute | solution.py:1133
  28.0 24.8 %collective-permute-start.9 = (bf16[4,48,768]{2,1,0:T(8,128)(2,1)S(1)}, bf16[4,48,768]{2,1,0:T(8,128)(2,1)S(1)}, u32[]{:S(2)}, u32[]{:S(2)}) collective-permute-start(bf16[4,48,768]{2,1,0:T(8,128)(2,1)S(1)} %slice.182), channel_id=1, source_target_pairs={{0,6},{2,4},{4,2},{6,0},{8,14},{10,12},{12,10},{14,8},{16,22},{18,... | collective-permute-start | bytes 884744 | tf_op jit(solution)/shard_map/ppermute | solution.py:1123
  29.7 23.2 %collective-permute-start.8 = (bf16[4,48,768]{2,1,0:T(8,128)(2,1)S(1)}, bf16[4,48,768]{2,1,0:T(8,128)(2,1)S(1)}, u32[]{:S(2)}, u32[]{:S(2)}) collective-permute-start(bf16[4,48,768]{2,1,0:T(8,128)(2,1)S(1)} %slice.182), channel_id=1, source_target_pairs={{0,4},{2,6},{4,0},{6,2},{8,12},{10,14},{12,8},{14,10},{16,20},{18,... | collective-permute-start | bytes 884744 | tf_op jit(solution)/shard_map/ppermute | solution.py:1123
  29.9 23.0 %collective-permute-start.7 = (bf16[4,48,768]{2,1,0:T(8,128)(2,1)S(1)}, bf16[4,48,768]{2,1,0:T(8,128)(2,1)S(1)}, u32[]{:S(2)}, u32[]{:S(2)}) collective-permute-start(bf16[4,48,768]{2,1,0:T(8,128)(2,1)S(1)} %slice.182), channel_id=1, source_target_pairs={{0,2},{2,0},{4,6},{6,4},{8,10},{10,8},{12,14},{14,12},{16,18},{18,... | collective-permute-start | bytes 884744 | tf_op jit(solution)/shard_map/ppermute | solution.py:1123
  52.8 3.8 %slice-start = ((f32[12,384]{1,0:T(8,128)}), f32[4,384]{1,0:T(4,128)S(1)}, s32[]{:S(2)}) async-start(f32[12,384]{1,0:T(8,128)} %vec_ref.5), calls=%async_computation.1 | async-start | bytes 12288 | tf_op jit(solution)/shard_map/slice | solution.py:1239
  55.8 3.6 %collective-permute-start.11 = (bf16[16,48,768]{2,1,0:T(8,128)(2,1)}, bf16[16,48,768]{2,1,0:T(8,128)(2,1)S(1)}, u32[]{:S(2)}, u32[]{:S(2)}) collective-permute-start(bf16[16,48,768]{2,1,0:T(8,128)(2,1)} %constant_dynamic-update-slice_fusion.ff0_ref), channel_id=1, source_target_pairs={{0,1},{1,0},{2,3},{3,2},{4,5},{5,4},{6,7},{7,6},{8,9},{9,8},{10,11... | collective-permute-start | bytes 3538952 | tf_op jit(solution)/shard_map/ppermute | solution.py:1133
  92.0 3.1 %collective-permute-start.12 = (bf16[768,768]{1,0:T(8,128)(2,1)}, bf16[768,768]{1,0:T(8,128)(2,1)S(1)}, u32[]{:S(2)}, u32[]{:S(2)}) collective-permute-start(bf16[768,768]{1,0:T(8,128)(2,1)} %get-tuple-element.96), channel_id=1, source_target_pairs={{0,1},{1,0},{2,3},{3,2},{4,5},{5,4},{6,7},{7,6},{8,9},{9,8},{10,11... | collective-permute-start | bytes 3538952 | tf_op jit(solution)/shard_map/ppermute | solution.py:1133
  97.5 35.9 %all-to-all-start = ((bf16[16,48,768]{2,1,0:T(8,128)(2,1)}), bf16[16,48,768]{2,1,0:T(8,128)(2,1)S(1)}, u32[]{:S(2)}, u32[]{:S(2)}) async-start(bf16[16,48,768]{2,1,0:T(8,128)(2,1)} %bitcast.14), calls=%async_computation | async-start | bytes 2359296 | tf_op jit(solution)/shard_map/all_to_all | solution.py:1137
  133.4 1.7 %copy-start.27 = (f32[384,48]{0,1:T(8,128)S(1)}, f32[384,48]{0,1:T(8,128)}, u32[]{:S(2)}) copy-start(f32[384,48]{0,1:T(8,128)} %param.42) | copy-start | bytes 221188
  133.4 2.6 %copy-start.18 = (bf16[17,24,768]{2,1,0:T(8,128)(2,1)S(1)}, bf16[17,24,768]{2,1,0:T(8,128)(2,1)}, u32[]{:S(2)}) copy-start(bf16[17,24,768]{2,1,0:T(8,128)(2,1)} %get-tuple-element.107) | copy-start | bytes 1880068
  133.4 2.6 %collective-permute-start.13 = (bf16[17,24,768]{2,1,0:T(8,128)(2,1)}, bf16[17,24,768]{2,1,0:T(8,128)(2,1)S(1)}, u32[]{:S(2)}, u32[]{:S(2)}) collective-permute-start(bf16[17,24,768]{2,1,0:T(8,128)(2,1)} %get-tuple-element.110), channel_id=1, source_target_pairs={{0,1},{1,0},{2,3},{3,2},{4,5},{5,4},{6,7},{7,6},{8,9},{9,8},{10,11... | collective-permute-start | bytes 1880072 | tf_op jit(solution)/shard_map/ppermute | solution.py:1133
  135.1 4.2 %copy-start.20 = (f32[48,384]{1,0:T(8,128)}, f32[48,384]{1,0:T(8,128)S(1)}, u32[]{:S(2)}) copy-start(f32[48,384]{1,0:T(8,128)S(1)} %get-tuple-element.131) | copy-start | bytes 221188
  135.8 15.1 %copy-start.21 = (f32[384,48]{0,1:T(8,128)}, f32[384,48]{0,1:T(8,128)S(1)}, u32[]{:S(2)}) copy-start(f32[384,48]{0,1:T(8,128)S(1)} %get-tuple-element.135) | copy-start | bytes 221188
  136.2 3.1 %copy-start.30 = (f32[48,384]{1,0:T(8,128)S(1)}, f32[48,384]{1,0:T(8,128)}, u32[]{:S(2)}) copy-start(f32[48,384]{1,0:T(8,128)} %param.57) | copy-start | bytes 221188
  136.3 6.0 %collective-permute-start.14 = (bf16[112,768]{1,0:T(8,128)(2,1)S(1)}, bf16[112,768]{1,0:T(8,128)(2,1)S(1)}, u32[]{:S(2)}, u32[]{:S(2)}) collective-permute-start(bf16[112,768]{1,0:T(8,128)(2,1)S(1)} %get-tuple-element.159), channel_id=1, source_target_pairs={{0,2},{2,0},{4,6},{6,4},{8,10},{10,8},{12,14},{14,12},{16,18},{18,... | collective-permute-start | bytes 516104 | tf_op jit(solution)/shard_map/ppermute | solution.py:1123
  138.0 9.0 %collective-permute-start.16 = (bf16[112,768]{1,0:T(8,128)(2,1)S(1)}, bf16[112,768]{1,0:T(8,128)(2,1)S(1)}, u32[]{:S(2)}, u32[]{:S(2)}) collective-permute-start(bf16[112,768]{1,0:T(8,128)(2,1)S(1)} %get-tuple-element.160), channel_id=1, source_target_pairs={{0,6},{2,4},{4,2},{6,0},{8,14},{10,12},{12,10},{14,8},{16,22},{18,... | collective-permute-start | bytes 516104 | tf_op jit(solution)/shard_map/ppermute | solution.py:1123
  139.2 7.9 %collective-permute-start.15 = (bf16[112,768]{1,0:T(8,128)(2,1)S(1)}, bf16[112,768]{1,0:T(8,128)(2,1)S(1)}, u32[]{:S(2)}, u32[]{:S(2)}) collective-permute-start(bf16[112,768]{1,0:T(8,128)(2,1)S(1)} %get-tuple-element.161), channel_id=1, source_target_pairs={{0,4},{2,6},{4,0},{6,2},{8,12},{10,14},{12,8},{14,10},{16,20},{18,... | collective-permute-start | bytes 516104 | tf_op jit(solution)/shard_map/ppermute | solution.py:1123
  147.1 3.8 %copy-start.31 = (f32[384,48]{0,1:T(8,128)S(1)}, f32[384,48]{0,1:T(8,128)}, u32[]{:S(2)}) copy-start(f32[384,48]{0,1:T(8,128)} %param.54) | copy-start | bytes 221188
  147.3 4.3 %collective-permute-start.17 = (bf16[40,768]{1,0:T(8,128)(2,1)S(1)}, bf16[40,768]{1,0:T(8,128)(2,1)S(1)}, u32[]{:S(2)}, u32[]{:S(2)}) collective-permute-start(bf16[40,768]{1,0:T(8,128)(2,1)S(1)} %get-tuple-element.156), channel_id=1, source_target_pairs={{0,8},{2,10},{4,12},{6,14},{8,0},{10,2},{12,4},{14,6},{16,24},{18,... | collective-permute-start | bytes 184328 | tf_op jit(solution)/shard_map/ppermute | solution.py:1123
  148.5 4.7 %collective-permute-start.18 = (bf16[40,768]{1,0:T(8,128)(2,1)S(1)}, bf16[40,768]{1,0:T(8,128)(2,1)S(1)}, u32[]{:S(2)}, u32[]{:S(2)}) collective-permute-start(bf16[40,768]{1,0:T(8,128)(2,1)S(1)} %get-tuple-element.157), channel_id=1, source_target_pairs={{0,16},{2,18},{4,20},{6,22},{8,24},{10,26},{12,28},{14,30},{16,0},... | collective-permute-start | bytes 184328 | tf_op jit(solution)/shard_map/ppermute | solution.py:1123
  150.6 5.6 %collective-permute-start.19 = (bf16[40,768]{1,0:T(8,128)(2,1)S(1)}, bf16[40,768]{1,0:T(8,128)(2,1)S(1)}, u32[]{:S(2)}, u32[]{:S(2)}) collective-permute-start(bf16[40,768]{1,0:T(8,128)(2,1)S(1)} %get-tuple-element.158), channel_id=1, source_target_pairs={{0,24},{2,26},{4,28},{6,30},{8,16},{10,18},{12,20},{14,22},{16,8},... | collective-permute-start | bytes 184328 | tf_op jit(solution)/shard_map/ppermute | solution.py:1123
  151.6 9.6 %copy-start.36 = (f32[6,530]{1,0:T(8,128)S(1)}, f32[6,530]{1,0:T(8,128)}, u32[]{:S(2)}) copy-start(f32[6,530]{1,0:T(8,128)} %param.60) | copy-start | bytes 38164
  151.6 9.6 %copy-start.37 = (f32[6,530]{1,0:T(8,128)S(1)}, f32[6,530]{1,0:T(8,128)}, u32[]{:S(2)}) copy-start(f32[6,530]{1,0:T(8,128)} %param.58) | copy-start | bytes 38164
  151.6 9.6 %copy-start.38 = (f32[6,530]{1,0:T(8,128)S(1)}, f32[6,530]{1,0:T(8,128)}, u32[]{:S(2)}) copy-start(f32[6,530]{1,0:T(8,128)} %param.59) | copy-start | bytes 38164
  151.6 10.3 %copy-start.3 = (f32[3,24,192]{2,1,0:T(8,128)S(1)}, f32[3,24,192]{2,1,0:T(8,128)}, u32[]{:S(2)}) copy-start(f32[3,24,192]{2,1,0:T(8,128)} %refs_0_.1) | copy-start | bytes 165892
  151.6 10.3 %copy-start.4 = (f32[3,24,192]{2,1,0:T(8,128)S(1)}, f32[3,24,192]{2,1,0:T(8,128)}, u32[]{:S(2)}) copy-start(f32[3,24,192]{2,1,0:T(8,128)} %refs_1_.1) | copy-start | bytes 165892
  151.6 10.3 %copy-start.5 = (f32[3,24,192]{2,1,0:T(8,128)S(1)}, f32[3,24,192]{2,1,0:T(8,128)}, u32[]{:S(2)}) copy-start(f32[3,24,192]{2,1,0:T(8,128)} %refs_2_.1) | copy-start | bytes 165892
  151.6 10.3 %copy-start.6 = (f32[3,24,192]{2,1,0:T(8,128)S(1)}, f32[3,24,192]{2,1,0:T(8,128)}, u32[]{:S(2)}) copy-start(f32[3,24,192]{2,1,0:T(8,128)} %refs_3_.1) | copy-start | bytes 165892
  151.6 10.3 %copy-start.7 = (f32[192,24]{0,1:T(8,128)S(1)}, f32[192,24]{0,1:T(8,128)}, u32[]{:S(2)}) copy-start(f32[192,24]{0,1:T(8,128)} %param.41) | copy-start | bytes 55300
  151.7 10.3 %copy-start.8 = (f32[192,24]{0,1:T(8,128)S(1)}, f32[192,24]{0,1:T(8,128)}, u32[]{:S(2)}) copy-start(f32[192,24]{0,1:T(8,128)} %param.49) | copy-start | bytes 55300
  151.7 10.3 %copy-start.9 = (f32[192,24]{0,1:T(8,128)S(1)}, f32[192,24]{0,1:T(8,128)}, u32[]{:S(2)}) copy-start(f32[192,24]{0,1:T(8,128)} %param.50) | copy-start | bytes 55300
  151.7 10.3 %copy-start.10 = (f32[192,24]{0,1:T(8,128)S(1)}, f32[192,24]{0,1:T(8,128)}, u32[]{:S(2)}) copy-start(f32[192,24]{0,1:T(8,128)} %param.51) | copy-start | bytes 55300
  156.6 6.2 %collective-permute-start.20 = (f32[3,768]{1,0:T(4,128)S(1)}, f32[3,768]{1,0:T(4,128)S(1)}, u32[]{:S(2)}, u32[]{:S(2)}) collective-permute-start(f32[3,768]{1,0:T(4,128)S(1)} %slice.260), channel_id=1, source_target_pairs={{0,1},{1,0},{2,3},{3,2},{4,5},{5,4},{6,7},{7,6},{8,9},{9,8},{10,11... | collective-permute-start | bytes 27656 | tf_op jit(solution)/shard_map/ppermute | solution.py:1133
  (16 other events, 18.4 us)
